TPU v7x, 512 devices: a whole 4x8x8 slice. The times are simulated.
512 devices in a mesh: section: 16 (over x, y_lo, core), bulk: 32 (over y_hi, z).
Axes of the slice: x: 4, y: 8 (y_hi: 4, y_lo: 2; y = y_hi * 2 + y_lo), z: 8, core: 2. Of those that a mesh axis runs over, the one named last changes fastest.
Arguments:
- activations: bfloat16 [16, 4, 8192, 256], P('section', None, 'bulk'), may hold values from -6 to 6
- weights: bfloat16 [16, 3, 256, 256], P('section'), may hold values from -0.109375 to 0.109375
- film_gain: float32 [16, 36, 256], P('section'), may hold values from 0.25 to 1.75
- film_shift: float32 [16, 36, 256], P('section'), may hold values from -3 to 3
- doa_bins: int32 [4], replicated, may hold values from 0 to 35
- cotangent: bfloat16 [4, 8192, 256], P(None, 'bulk'), may hold values from -6 to 6
Outputs:
- d_inputs: bfloat16 [16, 4, 8192, 256], P('section', None, 'bulk')
- d_weights: float32 [16, 3, 256, 256], P('section')
- d_gain: float32 [16, 36, 256], P('section')
- d_shift: float32 [16, 36, 256], P('section')
All inputs are finite; a program needn't handle non-finite values.
Results may differ from a plain program's by a relative error of at most 0.014.
Values may be sent and summed in bfloat16 or wider, within the bound.
A program may use at most 64 MiB of HBM per device.

v0:
```python
import jax
import jax.numpy as jnp
from jax import lax
from jax.sharding import PartitionSpec as P


def passed_along(value, axis, steps):
    count = lax.axis_size(axis)
    first, last = (max(0, -steps), min(count, count - steps))
    return lax.ppermute(value, axis, [(source, source + steps) for source in range(first, last)])


def extended(block, sides, width):
    for axis, dim in sides:
        count = lax.axis_size(axis)
        forward = [(i, i + 1) for i in range(count - 1)]
        forward.append((count - 1, 0))
        backward = [(target, source) for source, target in forward]
        low = lax.ppermute(
            lax.slice_in_dim(block, block.shape[dim] - width, None, axis=dim), axis, forward
        )
        high = lax.ppermute(lax.slice_in_dim(block, 0, width, axis=dim), axis, backward)
        block = jnp.concatenate([low, block, high], axis=dim)
    return block


def times_trans(left, right):
    return lax.dot_general(
        left, right, (((1,), (1,)), ((), ())), preferred_element_type=jnp.float32
    )


def trans_times(left, right):
    return lax.dot_general(
        left, right, (((0,), (0,)), ((), ())), preferred_element_type=jnp.float32
    )


def shards(activations, weights, film_gain, film_shift, doa_bins, cotangent):
    sections = lax.axis_size("section")
    section_id = lax.axis_index("section")
    micro_count = activations.shape[1]
    row_total = activations.shape[2]
    channels = activations.shape[3]
    bins_count = film_gain.shape[1]
    local_acts = activations[0]
    w_set = weights[0]
    gain_table = film_gain[0]
    shift_table = film_shift[0]

    def step_fn(step_now, state_now):
        sent, grad_w, grad_gain, grad_shift, d_local = state_now
        received = passed_along(sent, "section", -1)
        step_index = step_now - (sections - 1 - section_id)
        is_active = (step_index >= 0) & (step_index < micro_count)
        slot_index = jnp.clip(step_index, 0, micro_count - 1)
        top_part = lax.dynamic_index_in_dim(cotangent, slot_index, 0, keepdims=False)
        incoming = jnp.where(section_id == sections - 1, top_part, received)
        act_now = lax.dynamic_index_in_dim(local_acts, slot_index, 0, keepdims=False)
        padded = extended(act_now, (("bulk", 0),), 1)
        before = padded[:-2]
        middle = padded[1:-1]
        after = padded[2:]
        pre_film = jnp.dot(before, w_set[0], preferred_element_type=jnp.float32)
        pre_film = pre_film + jnp.dot(middle, w_set[1], preferred_element_type=jnp.float32)
        pre_film = pre_film + jnp.dot(after, w_set[2], preferred_element_type=jnp.float32)
        bin_id = lax.dynamic_index_in_dim(doa_bins, slot_index, 0, keepdims=False)
        onehot = (lax.iota(jnp.int32, bins_count) == bin_id).astype(jnp.float32)
        gain_row = jnp.dot(onehot, gain_table, precision=lax.Precision.HIGHEST)
        shift_row = jnp.dot(onehot, shift_table, precision=lax.Precision.HIGHEST)
        filmed = pre_film * gain_row + shift_row
        sigmoid_v = jax.nn.sigmoid(filmed)
        top_grad = incoming.astype(jnp.float32)
        grad_film = top_grad * sigmoid_v * (1.0 + filmed * (1.0 - sigmoid_v))
        grad_pre = (grad_film * gain_row).astype(jnp.bfloat16)
        grad_ext = extended(grad_pre, (("bulk", 0),), 1)
        grad_input = (
            top_grad + times_trans(grad_ext[2:], w_set[0]) + times_trans(grad_pre, w_set[1])
        )
        grad_input = grad_input + times_trans(grad_ext[:-2], w_set[2])
        grad_input = grad_input.astype(jnp.bfloat16)
        w_term = jnp.stack(
            [
                trans_times(before, grad_pre),
                trans_times(middle, grad_pre),
                trans_times(after, grad_pre),
            ]
        )
        grad_w = grad_w + jnp.where(is_active, w_term, 0.0)
        gain_term = onehot[:, None] * jnp.sum(grad_film * pre_film, 0)[None, :]
        shift_term = onehot[:, None] * jnp.sum(grad_film, 0)[None, :]
        grad_gain = grad_gain + jnp.where(is_active, gain_term, 0.0)
        grad_shift = grad_shift + jnp.where(is_active, shift_term, 0.0)
        new_sent = jnp.where(is_active, grad_input, jnp.zeros_like(grad_input))
        existing = lax.dynamic_index_in_dim(d_local, slot_index, 0, keepdims=False)
        d_local = lax.dynamic_update_index_in_dim(
            d_local, jnp.where(is_active, grad_input, existing), slot_index, 0
        )
        return (new_sent, grad_w, grad_gain, grad_shift, d_local)

    start_state = (
        jnp.zeros((row_total, channels), jnp.bfloat16),
        jnp.zeros((3, channels, channels), jnp.float32),
        jnp.zeros((bins_count, channels), jnp.float32),
        jnp.zeros((bins_count, channels), jnp.float32),
        jnp.zeros((micro_count, row_total, channels), jnp.bfloat16),
    )
    final_state = lax.fori_loop(0, sections + micro_count - 1, step_fn, start_state)
    sent_last, grad_w, grad_gain, grad_shift, d_local = final_state
    whole_w, sum_gain, sum_shift = lax.psum((grad_w, grad_gain, grad_shift), "bulk")
    return (d_local[None], whole_w[None], sum_gain[None], sum_shift[None])


def solution(mesh):
    return jax.shard_map(
        shards,
        mesh=mesh,
        in_specs=(
            P("section", None, "bulk", None),
            P("section", None, None, None),
            P("section", None, None),
            P("section", None, None),
            P(),
            P(None, "bulk", None),
        ),
        out_specs=(
            P("section", None, "bulk", None),
            P("section", None, None, None),
            P("section", None, None),
            P("section", None, None),
        ),
        check_vma=False,
    )
```

profile of v0, /device:TPU:2, one launch (start us, length us, event | category | flops | bytes accessed | tf_op | source)
XLA Modules:
  0.0 1215.6 jit_solution(6824200774227903969)
XLA Ops:
  8.8 601.1 %while.24 = (s32[]{:T(128)}, bf16[256,256]{1,0:T(8,128)(2,1)S(1)}, f32[3,256,256]{2,1,0:T(8,128)S(1)}, f32[36,256]{1,0:T(8,128)S(1)}, f32[36,256]{1,0:T(8,128)S(...) while((s32[]{:T(128)}, bf16[256,256]{1,0:T(8,128)(2,1)S(1)}, ...), condition=%wide.region_3.4_spmd.clone, body=%wide.region_0.3_spmd.clone.sunk | while | flops 306675328 | bytes 13093692 | solution.py:108
  9.5 14.6 %collective-permute-start.1 = (bf16[1,256]{1,0:T(2,128)(2,1)S(1)}, bf16[1,256]{1,0:T(2,128)(2,1)S(1)}, u32[]{:S(2)}, u32[]{:S(2)}) collective-permute-start(bf16[1,256]{1,0:T(2,128)(2,1)S(1)} %get-tuple-element.496), channel_id=1, source_target_pairs={{1,0},{2,1},{3,2},{4,3},{5,4},{6,5},{7,6},{8,7},{9,8},{10,9},{11,1... | collective-permute-start | bytes 1544 | tf_op jit(solution)/shard_map/while/body/eval_jaxpr/ppermute | solution.py:22
  24.1 1.9 collective-permute-start.2
  34.6 1.9 collective-permute-start.3
  36.6 8.1 collective-permute-start.4
  47.0 8.4 collective-permute-start.1
  55.4 1.9 collective-permute-start.2
  57.4 1.9 collective-permute-start
  67.9 8.1 collective-permute-start.4
  78.3 8.4 collective-permute-start.1
  99.2 8.1 collective-permute-start.4
  109.7 8.4 collective-permute-start.1
  128.6 1.9 collective-permute-start.3
  130.5 8.1 collective-permute-start.4
  141.0 8.4 collective-permute-start.1
  161.8 8.1 collective-permute-start.4
  172.3 8.4 collective-permute-start.1
  193.1 8.1 collective-permute-start.4
  203.6 8.4 collective-permute-start.1
  222.5 1.9 collective-permute-start.3
  224.4 8.1 collective-permute-start.4
  234.9 8.4 collective-permute-start.1
  255.7 8.1 collective-permute-start.4
  266.2 8.4 collective-permute-start.1
  287.1 8.1 collective-permute-start.4
  297.5 8.4 collective-permute-start.1
  318.4 8.1 collective-permute-start.4
  328.8 8.4 collective-permute-start.1
  349.7 8.1 collective-permute-start.4
  360.1 8.4 collective-permute-start.1
  381.0 8.1 collective-permute-start.4
  391.4 8.4 collective-permute-start.1
  412.3 8.1 collective-permute-start.4
  422.8 8.4 collective-permute-start.1
  443.6 8.1 collective-permute-start.4
  454.1 8.4 collective-permute-start.1
  474.9 8.1 collective-permute-start.4
  485.4 8.4 collective-permute-start.1
  506.2 8.1 collective-permute-start.4
  516.7 8.4 collective-permute-start.1
  537.5 8.1 collective-permute-start.4
  548.0 8.4 collective-permute-start.1
  568.8 8.1 collective-permute-start.4
  579.3 8.4 collective-permute-start.1
  600.1 8.1 collective-permute-start.4
  612.0 275.1 %all-reduce.6.cloned.1.call-done = (f32[1,36,256]{2,0,1:T(1,128)}, f32[1,36,256]{2,0,1:T(1,128)}) async-done(((f32[1,36,256]{2,0,1:T(1,128)}, f32[1,36,256]{2,0,1:T(1,128)}), (f32[1,36,256]{2,0,1:T(1,128)}, f32[1,36,256]{2,0,1:T(1,128)})) %all-reduce.6.cloned.1.call-update) | async-done | bytes 73744 | tf_op jit(solution)/shard_map/psum | solution.py:110
  887.1 318.1 %all-reduce.4.cloned.1.call-done = f32[1,3,256,256]{3,2,1,0:T(8,128)} async-done(((f32[1,3,256,256]{3,2,1,0:T(8,128)}), f32[1,3,256,256]{3,2,1,0:T(8,128)}) %all-reduce.4.cloned.1.call-update) | async-done | bytes 786448 | tf_op jit(solution)/shard_map/psum | solution.py:110
  1205.2 2.1 copy.36
  (628 shorter events, 270.2 us)
Async XLA Ops:
  7.2 880.0 %all-reduce.6.cloned.1.call-start = ((), (), s32[]{:S(2)}) async-start(), calls=%async_computation.1 | async-start | bytes 147456 | tf_op jit(solution)/shard_map/psum | solution.py:110
  9.5 22.5 %collective-permute-start.1 = (bf16[1,256]{1,0:T(2,128)(2,1)S(1)}, bf16[1,256]{1,0:T(2,128)(2,1)S(1)}, u32[]{:S(2)}, u32[]{:S(2)}) collective-permute-start(bf16[1,256]{1,0:T(2,128)(2,1)S(1)} %get-tuple-element.496), channel_id=1, source_target_pairs={{1,0},{2,1},{3,2},{4,3},{5,4},{6,5},{7,6},{8,7},{9,8},{10,9},{11,1... | collective-permute-start | bytes 1544 | tf_op jit(solution)/shard_map/while/body/eval_jaxpr/ppermute | solution.py:22
  24.1 9.7 collective-permute-start.2
  34.6 10.9 collective-permute-start.3
  47.0 16.2 %collective-permute-start.1 = (bf16[1,256]{1,0:T(2,128)(2,1)S(1)}, bf16[1,256]{1,0:T(2,128)(2,1)S(1)}, u32[]{:S(2)}, u32[]{:S(2)}) collective-permute-start(bf16[1,256]{1,0:T(2,128)(2,1)S(1)} %get-tuple-element.496), channel_id=1, source_target_pairs={{1,0},{2,1},{3,2},{4,3},{5,4},{6,5},{7,6},{8,7},{9,8},{10,9},{11,1... | collective-permute-start | bytes 1544 | tf_op jit(solution)/shard_map/while/body/eval_jaxpr/ppermute | solution.py:22
  55.4 9.7 collective-permute-start.2
  65.9 10.9 collective-permute-start.3
  78.3 16.2 %collective-permute-start.1 = (bf16[1,256]{1,0:T(2,128)(2,1)S(1)}, bf16[1,256]{1,0:T(2,128)(2,1)S(1)}, u32[]{:S(2)}, u32[]{:S(2)}) collective-permute-start(bf16[1,256]{1,0:T(2,128)(2,1)S(1)} %get-tuple-element.496), channel_id=1, source_target_pairs={{1,0},{2,1},{3,2},{4,3},{5,4},{6,5},{7,6},{8,7},{9,8},{10,9},{11,1... | collective-permute-start | bytes 1544 | tf_op jit(solution)/shard_map/while/body/eval_jaxpr/ppermute | solution.py:22
  86.7 9.7 collective-permute-start.2
  97.3 10.9 collective-permute-start.3
  109.7 16.2 %collective-permute-start.1 = (bf16[1,256]{1,0:T(2,128)(2,1)S(1)}, bf16[1,256]{1,0:T(2,128)(2,1)S(1)}, u32[]{:S(2)}, u32[]{:S(2)}) collective-permute-start(bf16[1,256]{1,0:T(2,128)(2,1)S(1)} %get-tuple-element.496), channel_id=1, source_target_pairs={{1,0},{2,1},{3,2},{4,3},{5,4},{6,5},{7,6},{8,7},{9,8},{10,9},{11,1... | collective-permute-start | bytes 1544 | tf_op jit(solution)/shard_map/while/body/eval_jaxpr/ppermute | solution.py:22
  118.0 9.7 collective-permute-start.2
  128.6 10.9 collective-permute-start.3
  141.0 16.2 %collective-permute-start.1 = (bf16[1,256]{1,0:T(2,128)(2,1)S(1)}, bf16[1,256]{1,0:T(2,128)(2,1)S(1)}, u32[]{:S(2)}, u32[]{:S(2)}) collective-permute-start(bf16[1,256]{1,0:T(2,128)(2,1)S(1)} %get-tuple-element.496), channel_id=1, source_target_pairs={{1,0},{2,1},{3,2},{4,3},{5,4},{6,5},{7,6},{8,7},{9,8},{10,9},{11,1... | collective-permute-start | bytes 1544 | tf_op jit(solution)/shard_map/while/body/eval_jaxpr/ppermute | solution.py:22
  149.4 9.7 collective-permute-start.2
  159.9 10.9 collective-permute-start.3
  172.3 16.2 %collective-permute-start.1 = (bf16[1,256]{1,0:T(2,128)(2,1)S(1)}, bf16[1,256]{1,0:T(2,128)(2,1)S(1)}, u32[]{:S(2)}, u32[]{:S(2)}) collective-permute-start(bf16[1,256]{1,0:T(2,128)(2,1)S(1)} %get-tuple-element.496), channel_id=1, source_target_pairs={{1,0},{2,1},{3,2},{4,3},{5,4},{6,5},{7,6},{8,7},{9,8},{10,9},{11,1... | collective-permute-start | bytes 1544 | tf_op jit(solution)/shard_map/while/body/eval_jaxpr/ppermute | solution.py:22
  180.7 9.7 collective-permute-start.2
  191.2 10.9 collective-permute-start.3
  203.6 16.2 %collective-permute-start.1 = (bf16[1,256]{1,0:T(2,128)(2,1)S(1)}, bf16[1,256]{1,0:T(2,128)(2,1)S(1)}, u32[]{:S(2)}, u32[]{:S(2)}) collective-permute-start(bf16[1,256]{1,0:T(2,128)(2,1)S(1)} %get-tuple-element.496), channel_id=1, source_target_pairs={{1,0},{2,1},{3,2},{4,3},{5,4},{6,5},{7,6},{8,7},{9,8},{10,9},{11,1... | collective-permute-start | bytes 1544 | tf_op jit(solution)/shard_map/while/body/eval_jaxpr/ppermute | solution.py:22
  212.0 9.7 collective-permute-start.2
  222.5 10.9 collective-permute-start.3
  234.9 16.2 %collective-permute-start.1 = (bf16[1,256]{1,0:T(2,128)(2,1)S(1)}, bf16[1,256]{1,0:T(2,128)(2,1)S(1)}, u32[]{:S(2)}, u32[]{:S(2)}) collective-permute-start(bf16[1,256]{1,0:T(2,128)(2,1)S(1)} %get-tuple-element.496), channel_id=1, source_target_pairs={{1,0},{2,1},{3,2},{4,3},{5,4},{6,5},{7,6},{8,7},{9,8},{10,9},{11,1... | collective-permute-start | bytes 1544 | tf_op jit(solution)/shard_map/while/body/eval_jaxpr/ppermute | solution.py:22
  243.3 9.7 collective-permute-start.2
  253.8 10.9 collective-permute-start.3
  266.2 16.2 %collective-permute-start.1 = (bf16[1,256]{1,0:T(2,128)(2,1)S(1)}, bf16[1,256]{1,0:T(2,128)(2,1)S(1)}, u32[]{:S(2)}, u32[]{:S(2)}) collective-permute-start(bf16[1,256]{1,0:T(2,128)(2,1)S(1)} %get-tuple-element.496), channel_id=1, source_target_pairs={{1,0},{2,1},{3,2},{4,3},{5,4},{6,5},{7,6},{8,7},{9,8},{10,9},{11,1... | collective-permute-start | bytes 1544 | tf_op jit(solution)/shard_map/while/body/eval_jaxpr/ppermute | solution.py:22
  285.1 10.9 collective-permute-start.3
  297.5 16.2 %collective-permute-start.1 = (bf16[1,256]{1,0:T(2,128)(2,1)S(1)}, bf16[1,256]{1,0:T(2,128)(2,1)S(1)}, u32[]{:S(2)}, u32[]{:S(2)}) collective-permute-start(bf16[1,256]{1,0:T(2,128)(2,1)S(1)} %get-tuple-element.496), channel_id=1, source_target_pairs={{1,0},{2,1},{3,2},{4,3},{5,4},{6,5},{7,6},{8,7},{9,8},{10,9},{11,1... | collective-permute-start | bytes 1544 | tf_op jit(solution)/shard_map/while/body/eval_jaxpr/ppermute | solution.py:22
  316.4 10.9 collective-permute-start.3
  328.8 16.2 %collective-permute-start.1 = (bf16[1,256]{1,0:T(2,128)(2,1)S(1)}, bf16[1,256]{1,0:T(2,128)(2,1)S(1)}, u32[]{:S(2)}, u32[]{:S(2)}) collective-permute-start(bf16[1,256]{1,0:T(2,128)(2,1)S(1)} %get-tuple-element.496), channel_id=1, source_target_pairs={{1,0},{2,1},{3,2},{4,3},{5,4},{6,5},{7,6},{8,7},{9,8},{10,9},{11,1... | collective-permute-start | bytes 1544 | tf_op jit(solution)/shard_map/while/body/eval_jaxpr/ppermute | solution.py:22
  347.7 10.9 collective-permute-start.3
  360.1 16.2 %collective-permute-start.1 = (bf16[1,256]{1,0:T(2,128)(2,1)S(1)}, bf16[1,256]{1,0:T(2,128)(2,1)S(1)}, u32[]{:S(2)}, u32[]{:S(2)}) collective-permute-start(bf16[1,256]{1,0:T(2,128)(2,1)S(1)} %get-tuple-element.496), channel_id=1, source_target_pairs={{1,0},{2,1},{3,2},{4,3},{5,4},{6,5},{7,6},{8,7},{9,8},{10,9},{11,1... | collective-permute-start | bytes 1544 | tf_op jit(solution)/shard_map/while/body/eval_jaxpr/ppermute | solution.py:22
  379.1 10.9 collective-permute-start.3
  391.4 16.2 %collective-permute-start.1 = (bf16[1,256]{1,0:T(2,128)(2,1)S(1)}, bf16[1,256]{1,0:T(2,128)(2,1)S(1)}, u32[]{:S(2)}, u32[]{:S(2)}) collective-permute-start(bf16[1,256]{1,0:T(2,128)(2,1)S(1)} %get-tuple-element.496), channel_id=1, source_target_pairs={{1,0},{2,1},{3,2},{4,3},{5,4},{6,5},{7,6},{8,7},{9,8},{10,9},{11,1... | collective-permute-start | bytes 1544 | tf_op jit(solution)/shard_map/while/body/eval_jaxpr/ppermute | solution.py:22
  410.4 10.9 collective-permute-start.3
  422.8 16.2 %collective-permute-start.1 = (bf16[1,256]{1,0:T(2,128)(2,1)S(1)}, bf16[1,256]{1,0:T(2,128)(2,1)S(1)}, u32[]{:S(2)}, u32[]{:S(2)}) collective-permute-start(bf16[1,256]{1,0:T(2,128)(2,1)S(1)} %get-tuple-element.496), channel_id=1, source_target_pairs={{1,0},{2,1},{3,2},{4,3},{5,4},{6,5},{7,6},{8,7},{9,8},{10,9},{11,1... | collective-permute-start | bytes 1544 | tf_op jit(solution)/shard_map/while/body/eval_jaxpr/ppermute | solution.py:22
  441.7 10.9 collective-permute-start.3
  454.1 16.2 %collective-permute-start.1 = (bf16[1,256]{1,0:T(2,128)(2,1)S(1)}, bf16[1,256]{1,0:T(2,128)(2,1)S(1)}, u32[]{:S(2)}, u32[]{:S(2)}) collective-permute-start(bf16[1,256]{1,0:T(2,128)(2,1)S(1)} %get-tuple-element.496), channel_id=1, source_target_pairs={{1,0},{2,1},{3,2},{4,3},{5,4},{6,5},{7,6},{8,7},{9,8},{10,9},{11,1... | collective-permute-start | bytes 1544 | tf_op jit(solution)/shard_map/while/body/eval_jaxpr/ppermute | solution.py:22
  473.0 10.9 collective-permute-start.3
  485.4 16.2 %collective-permute-start.1 = (bf16[1,256]{1,0:T(2,128)(2,1)S(1)}, bf16[1,256]{1,0:T(2,128)(2,1)S(1)}, u32[]{:S(2)}, u32[]{:S(2)}) collective-permute-start(bf16[1,256]{1,0:T(2,128)(2,1)S(1)} %get-tuple-element.496), channel_id=1, source_target_pairs={{1,0},{2,1},{3,2},{4,3},{5,4},{6,5},{7,6},{8,7},{9,8},{10,9},{11,1... | collective-permute-start | bytes 1544 | tf_op jit(solution)/shard_map/while/body/eval_jaxpr/ppermute | solution.py:22
  504.3 10.9 collective-permute-start.3
  516.7 16.2 %collective-permute-start.1 = (bf16[1,256]{1,0:T(2,128)(2,1)S(1)}, bf16[1,256]{1,0:T(2,128)(2,1)S(1)}, u32[]{:S(2)}, u32[]{:S(2)}) collective-permute-start(bf16[1,256]{1,0:T(2,128)(2,1)S(1)} %get-tuple-element.496), channel_id=1, source_target_pairs={{1,0},{2,1},{3,2},{4,3},{5,4},{6,5},{7,6},{8,7},{9,8},{10,9},{11,1... | collective-permute-start | bytes 1544 | tf_op jit(solution)/shard_map/while/body/eval_jaxpr/ppermute | solution.py:22
  535.6 10.9 collective-permute-start.3
  548.0 16.2 %collective-permute-start.1 = (bf16[1,256]{1,0:T(2,128)(2,1)S(1)}, bf16[1,256]{1,0:T(2,128)(2,1)S(1)}, u32[]{:S(2)}, u32[]{:S(2)}) collective-permute-start(bf16[1,256]{1,0:T(2,128)(2,1)S(1)} %get-tuple-element.496), channel_id=1, source_target_pairs={{1,0},{2,1},{3,2},{4,3},{5,4},{6,5},{7,6},{8,7},{9,8},{10,9},{11,1... | collective-permute-start | bytes 1544 | tf_op jit(solution)/shard_map/while/body/eval_jaxpr/ppermute | solution.py:22
  566.9 10.9 collective-permute-start.3
  579.3 16.2 %collective-permute-start.1 = (bf16[1,256]{1,0:T(2,128)(2,1)S(1)}, bf16[1,256]{1,0:T(2,128)(2,1)S(1)}, u32[]{:S(2)}, u32[]{:S(2)}) collective-permute-start(bf16[1,256]{1,0:T(2,128)(2,1)S(1)} %get-tuple-element.496), channel_id=1, source_target_pairs={{1,0},{2,1},{3,2},{4,3},{5,4},{6,5},{7,6},{8,7},{9,8},{10,9},{11,1... | collective-permute-start | bytes 1544 | tf_op jit(solution)/shard_map/while/body/eval_jaxpr/ppermute | solution.py:22
  598.2 10.9 collective-permute-start.3
  611.3 593.9 %all-reduce.4.cloned.1.call-start = ((), (), s32[]{:S(2)}) async-start(), calls=%async_computation | async-start | bytes 1572864 | tf_op jit(solution)/shard_map/psum | solution.py:110
  (74 other events, 1087.5 us)
Sparse Core Ops, SparseCore 0:
  611.4 275.6 all-reduce.5
  890.9 314.3 all-reduce.3
where the time goes:
time: 1220 us
  waiting for transfers between devices  630 us (52%)
  starting transfers between devices  430 us (35%)
  matrix products  68.4 us (6%)
  local copies, waits for them, and re-layouts  49.1 us (4%)
  other arithmetic  20.4 us (2%)
  between operations  14.1 us (1%)
    psum x2, waiting for transfers between devices, shards(): lax.psum((grad_w, grad_gain, grad_shift), 'bulk')  593 us
    ppermute x38, starting transfers between devices, extended(): lax.ppermute(lax.slice_in_dim(block, 0, width, axis=dim), axis, backward)  320 us
    ppermute x38, starting transfers between devices, extended(): lax.ppermute(lax.slice_in_dim(block, block.shape[dim] - width, None, axis...  73 us
    ppermute x19, starting transfers between devices, passed_along(): lax.ppermute(value, axis, [(source, source + steps) for source in range(f...  36.5 us
    ppermute x38, waiting for transfers between devices, extended(): lax.ppermute(lax.slice_in_dim(block, block.shape[dim] - width, None, axis...  31.4 us
  transfers between devices with their start and end apart: 97, of which 40 were waited for; matrix products, arithmetic and copies ran while one was open for 8% of the time, Pallas kernels for 0%

commit v1 on v0

v1 whole, which is shorter than its diff:
```python
import functools

import jax
import jax.numpy as jnp
from jax import lax
from jax.experimental import pallas as pl
from jax.experimental.pallas import tpu as pltpu
from jax.sharding import PartitionSpec as P

MESH = pl.DeviceIdType.MESH
F32 = jnp.float32
BF16 = jnp.bfloat16


def rolled(value, shift):
    return pltpu.roll(value, shift % value.shape[0], 0)


def body(sizes, x_ref, w_ref, gain_ref, shift_ref, bins_ref, cot_ref,
         din_ref, dw_ref, dgain_ref, dshift_ref,
         xh, wt, xt, gbuf, obuf, gpre, dgrad, dfull, dpre, acc, small,
         wpart, wland, wsum, wgather, sland, ssum,
         hx_s, hx_r, hc_s, hc_r, ch_s, ch_r, z_s, z_r, zs_s, zs_r, y_s, y_r, ys_s, ys_r, ag_s, ag_r):
    sections, nz, ny, micro, rows, channels, halo = sizes
    bulk = nz * ny
    ext = rows + 2 * halo
    wide = 2 * halo
    blk = 3 * channels // nz
    s = lax.axis_index("section")
    b = lax.axis_index("bulk")
    z = lax.rem(b, nz)
    y = b // nz
    left = lax.rem(b + bulk - 1, bulk)
    right = lax.rem(b + 1, bulk)
    is_last = s == sections - 1

    def z_peer(k):
        return y * nz + lax.rem(z + k, nz)

    def y_peer(k):
        return lax.rem(y + k, ny) * nz + z

    barrier = pltpu.get_barrier_semaphore()

    def greet(sec, blk_id):
        pl.semaphore_signal(barrier, inc=1, device_id=(sec, blk_id), device_id_type=MESH)

    greet(s, left)
    greet(s, right)
    for k in range(1, nz):
        greet(s, z_peer(k))
    for k in range(1, ny):
        greet(s, y_peer(k))

    @pl.when(s > 0)
    def _():
        greet(s - 1, b)

    @pl.when(s < sections - 1)
    def _():
        greet(s + 1, b)

    for k in range(3):
        wt[k] = w_ref[0, k].astype(F32).T.astype(BF16)
    for m in range(micro):
        xh[m, wide:wide + rows] = x_ref[0, m]

    @pl.when(is_last)
    def _():
        for m in range(micro):
            gbuf[m, halo:halo + rows] = cot_ref[m]

    base = 2 + (nz - 1) + (ny - 1)

    chain_peers = jnp.where(s > 0, 1, 0) + jnp.where(is_last, 0, 1)
    pl.semaphore_wait(barrier, base + chain_peers)

    def copy(src, dst, send, recv, to):
        return pltpu.make_async_remote_copy(src_ref=src, dst_ref=dst, send_sem=send, recv_sem=recv, device_id=to, device_id_type=MESH)

    x_right = copy(x_ref.at[0, :, pl.ds(rows - wide, wide)], xh.at[:, pl.ds(0, wide)], hx_s.at[0], hx_r.at[0], (s, right))
    x_left = copy(x_ref.at[0, :, pl.ds(0, wide)], xh.at[:, pl.ds(wide + rows, wide)], hx_s.at[1], hx_r.at[1], (s, left))
    c_right = copy(cot_ref.at[:, pl.ds(rows - halo, halo)], gbuf.at[:, pl.ds(0, halo)], hc_s.at[0], hc_r.at[0], (s, right))
    c_left = copy(cot_ref.at[:, pl.ds(0, halo)], gbuf.at[:, pl.ds(halo + rows, halo)], hc_s.at[1], hc_r.at[1], (s, left))
    x_right.start()
    x_left.start()

    @pl.when(is_last)
    def _():
        c_right.start()
        c_left.start()

    x_right.wait()
    x_left.wait()

    def forward(m, carry):
        xs = xh[m]
        pre = rolled(jnp.dot(xs, w_ref[0, 0], preferred_element_type=F32), 1)
        pre = pre + jnp.dot(xs, w_ref[0, 1], preferred_element_type=F32)
        pre = pre + rolled(jnp.dot(xs, w_ref[0, 2], preferred_element_type=F32), -1)
        pre = pre[halo:halo + ext]
        k = bins_ref[m]
        gain = gain_ref[0, pl.ds(k, 1), :]
        filmed = pre * gain + shift_ref[0, pl.ds(k, 1), :]
        sig = jax.nn.sigmoid(filmed)
        d = sig * (1.0 + filmed * (1.0 - sig))
        dfull[m] = d * gain
        d = d[halo:halo + rows]
        dgrad[m] = d
        dpre[m] = d * pre[halo:halo + rows]
        return carry

    lax.fori_loop(0, micro, forward, 0)

    def turn(m, carry):
        xs = xh[m].astype(F32)
        for j, sh in enumerate((1, 0, -1)):
            part = rolled(xs, sh) if sh else xs
            xt[m, j * channels:(j + 1) * channels] = part[wide:wide + rows].T.astype(BF16)
        return carry

    acc[...] = jnp.zeros_like(acc)

    def weight_step(m, carry):
        acc[...] += jnp.dot(xt[m], gpre[m, halo:halo + rows], preferred_element_type=F32)
        g = gbuf[m, halo:halo + rows].astype(F32)
        small[0, pl.ds(m, 1)] = jnp.sum(g * dpre[m], 0, keepdims=True)
        small[0, pl.ds(micro + m, 1)] = jnp.sum(g * dgrad[m], 0, keepdims=True)
        return carry

    @pl.when(jnp.logical_not(is_last))
    def _():
        lax.fori_loop(0, micro, turn, 0)

    @pl.when(is_last)
    def _():
        c_right.wait()
        c_left.wait()

    def chain_copy(m):
        return copy(obuf.at[m], gbuf.at[m], ch_s.at[m], ch_r.at[m], (s - 1, b))

    def chain(m, carry):
        @pl.when(jnp.logical_not(is_last))
        def _():
            chain_copy(m).wait_recv()

        g = gbuf[m].astype(F32)
        gp = (g * dfull[m]).astype(BF16)
        gpre[m] = gp
        out = g + jnp.dot(gp, wt[1], preferred_element_type=F32)
        out = out + rolled(jnp.dot(gp, wt[0], preferred_element_type=F32), -1)
        out = out + rolled(jnp.dot(gp, wt[2], preferred_element_type=F32), 1)
        obuf[m] = out.astype(BF16)

        @pl.when(s > 0)
        def _():
            chain_copy(m).start()

        @pl.when(jnp.logical_not(is_last))
        def _():
            weight_step(m, 0)

        return carry

    lax.fori_loop(0, micro, chain, 0)

    @pl.when(is_last)
    def _():
        lax.fori_loop(0, micro, turn, 0)
        lax.fori_loop(0, micro, weight_step, 0)

    for j in range(nz):
        wpart[j] = acc[j * blk:(j + 1) * blk].astype(BF16)

    def scatter(k):
        to = lax.rem(z + k, nz)
        return copy(wpart.at[to], wland.at[k], z_s.at[k], z_r.at[k], (s, y * nz + to))

    def small_z(k):
        return copy(small.at[0], sland.at[k], zs_s.at[k], zs_r.at[k], (s, z_peer(k)))

    for k in range(1, nz):
        scatter(k).start()
        small_z(k).start()

    for m in range(micro):
        din_ref[0, m] = obuf[m, halo:halo + rows]

    total = wpart[z].astype(F32)
    for k in range(1, nz):
        scatter(k).wait_recv()
        total = total + wland[k].astype(F32)
    wsum[y] = total.astype(BF16)

    def across(k):
        return copy(wsum.at[y], wsum.at[y], y_s.at[k], y_r.at[k], (s, y_peer(k)))

    for k in range(1, ny):
        across(k).start()

    sland[0] = small[0]
    for k in range(1, nz):
        small_z(k).wait_recv()
    tiny = sland[lax.rem(z, nz)]
    for j in range(1, nz):
        tiny = tiny + sland[lax.rem(z + nz - j, nz)]
    ssum[y] = tiny

    def small_y(k):
        return copy(ssum.at[y], ssum.at[y], ys_s.at[k], ys_r.at[k], (s, y_peer(k)))

    for k in range(1, ny):
        small_y(k).start()

    for k in range(1, ny):
        across(k).wait_recv()
    total = wsum[0].astype(F32)
    for j in range(1, ny):
        total = total + wsum[j].astype(F32)
    wgather[z] = total.astype(BF16)

    def gather(k):
        return copy(wgather.at[z], wgather.at[z], ag_s.at[k], ag_r.at[k], (s, z_peer(k)))

    for k in range(1, nz):
        gather(k).start()

    for k in range(1, ny):
        small_y(k).wait_recv()
    tiny = ssum[0]
    for j in range(1, ny):
        tiny = tiny + ssum[j]
    bins_count = dgain_ref.shape[1]
    spot = lax.broadcasted_iota(jnp.int32, (bins_count, channels), 0)
    out_gain = jnp.zeros((bins_count, channels), F32)
    out_shift = jnp.zeros((bins_count, channels), F32)
    for m in range(micro):
        hit = spot == bins_ref[m]
        out_gain = out_gain + jnp.where(hit, tiny[m:m + 1], 0.0)
        out_shift = out_shift + jnp.where(hit, tiny[micro + m:micro + m + 1], 0.0)
    dgain_ref[0] = out_gain
    dshift_ref[0] = out_shift

    for k in range(1, nz):
        gather(k).wait_recv()
    for j in range(nz):
        dw_ref[0, j * blk:(j + 1) * blk] = wgather[j].astype(F32)

    for k in range(1, nz):
        scatter(k).wait_send()
        small_z(k).wait_send()
        gather(k).wait_send()
    for k in range(1, ny):
        across(k).wait_send()
        small_y(k).wait_send()

    @pl.when(s > 0)
    def _():
        for m in range(micro):
            chain_copy(m).wait_send()


def shards(sections, bulk, activations, weights, film_gain, film_shift, doa_bins, cotangent):
    micro, rows, channels = activations.shape[1:]
    bins_count = film_gain.shape[1]
    nz = 8 if bulk == 32 else 2
    ny = bulk // nz
    halo = 16
    ext = rows + 2 * halo
    blk = 3 * channels // nz
    sizes = (sections, nz, ny, micro, rows, channels, halo)
    dma = pltpu.SemaphoreType.DMA
    vmem = pl.BlockSpec(memory_space=pltpu.VMEM)
    outs = pl.pallas_call(
        functools.partial(body, sizes),
        out_shape=(
            jax.ShapeDtypeStruct((1, micro, rows, channels), BF16),
            jax.ShapeDtypeStruct((1, 3 * channels, channels), F32),
            jax.ShapeDtypeStruct((1, bins_count, channels), F32),
            jax.ShapeDtypeStruct((1, bins_count, channels), F32),
        ),
        in_specs=[vmem, vmem, vmem, vmem, pl.BlockSpec(memory_space=pltpu.SMEM), vmem],
        out_specs=(vmem, vmem, vmem, vmem),
        scratch_shapes=[
            pltpu.VMEM((micro, ext + 2 * halo, channels), BF16),
            pltpu.VMEM((3, channels, channels), BF16),
            pltpu.VMEM((micro, 3 * channels, rows), BF16),
            pltpu.VMEM((micro, ext, channels), BF16),
            pltpu.VMEM((micro, ext, channels), BF16),
            pltpu.VMEM((micro, ext, channels), BF16),
            pltpu.VMEM((micro, rows, channels), F32),
            pltpu.VMEM((micro, ext, channels), F32),
            pltpu.VMEM((micro, rows, channels), F32),
            pltpu.VMEM((3 * channels, channels), F32),
            pltpu.VMEM((1, 2 * micro, channels), F32),
            pltpu.VMEM((nz, blk, channels), BF16),
            pltpu.VMEM((nz, blk, channels), BF16),
            pltpu.VMEM((ny, blk, channels), BF16),
            pltpu.VMEM((nz, blk, channels), BF16),
            pltpu.VMEM((nz, 2 * micro, channels), F32),
            pltpu.VMEM((ny, 2 * micro, channels), F32),
            dma((2,)), dma((2,)), dma((2,)), dma((2,)), dma((micro,)), dma((micro,)),
            dma((nz,)), dma((nz,)), dma((nz,)), dma((nz,)), dma((ny,)), dma((ny,)), dma((ny,)), dma((ny,)),
            dma((nz,)), dma((nz,)),
        ],
        compiler_params=pltpu.CompilerParams(
            collective_id=0, has_side_effects=True, vmem_limit_bytes=48 * 1024 * 1024
        ),
    )(activations, weights, film_gain, film_shift, doa_bins, cotangent)
    d_in, d_w, d_gain, d_shift = outs
    return d_in, d_w.reshape(1, 3, channels, channels), d_gain, d_shift


def solution(mesh):
    return jax.shard_map(
        functools.partial(shards, mesh.shape["section"], mesh.shape["bulk"]),
        mesh=mesh,
        in_specs=(
            P("section", None, "bulk", None),
            P("section", None, None, None),
            P("section", None, None),
            P("section", None, None),
            P(),
            P(None, "bulk", None),
        ),
        out_specs=(
            P("section", None, "bulk", None),
            P("section", None, None, None),
            P("section", None, None),
            P("section", None, None),
        ),
        check_vma=False,
    )
```

time: 1220 us -> 104 us (0.09)
  the two profiles are of different devices: /device:TPU:2 before, /device:TPU:1 now
where the time goes in v1:
time: 104 us; the launch traced here: 103 us
  Pallas kernels  94.8 us (91%)
  local copies, waits for them, and re-layouts  7.49 us (7%)
    pallas_call x1, Pallas kernels, shards(): pl.pallas_call(functools.partial(body, sizes), out_shape=(jax.ShapeDtypeS...  94.8 us
    unnamed x16, local copies, waits for them, and re-layouts  7.49 us

profile of v1, /device:TPU:1, one launch (start us, length us, event | category | flops | bytes accessed | tf_op | source)
XLA Modules:
  0.0 102.9 jit_solution(8538575095450567658)
XLA Ops:
  0.6 0.0 copy-start.4
  0.6 0.8 copy.10.gain_ref
  1.4 0.0 copy-done.4
  1.4 0.0 copy-start.3
  1.4 0.6 copy-done.3
  2.1 0.0 copy-start
  2.1 1.0 %copy-done = bf16[1,4,256,256]{3,2,1,0:T(8,128)(2,1)S(1)} copy-done((bf16[1,4,256,256]{3,2,1,0:T(8,128)(2,1)S(1)}, bf16[1,4,256,256]{3,2,1,0:T(8,128)(2,1)}, u32[]{:S(2)}) %copy-start) | copy-done | bytes 524312
  3.1 0.0 copy-start.1
  3.1 1.0 %copy-done.1 = bf16[4,256,256]{2,1,0:T(8,128)(2,1)S(1)} copy-done((bf16[4,256,256]{2,1,0:T(8,128)(2,1)S(1)}, bf16[4,256,256]{2,1,0:T(8,128)(2,1)}, u32[]{:S(2)}) %copy-start.1) | copy-done | bytes 524312
  4.2 0.0 copy-start.2
  4.2 1.0 copy-done.2
  5.2 94.8 %shard_map.93 = (bf16[1,4,256,256]{3,2,1,0:T(8,128)(2,1)S(1)}, f32[1,768,256]{2,1,0:T(8,128)S(1)}, f32[1,36,256]{2,1,0:T(8,128)S(1)}, f32[1,36,256]{2,1,0:T(8,128)S(1)}) custom-call(bf16[1,4,256,256]{3,2,1,0:T(8,128)(2,1)S(1)} %copy-done, bf16[1,3,256,256]{3,2,1,0:T(8,128)(2,1)S(1)} %copy-done.2, f32[1,36,256]{2,1,0:T(8,128)S(1)} %copy.10.gain_ref, ...), custom_call_target="tpu_custom_call" | custom-call | tf_op jit(solution)/shard_map/pallas_call | solution.py:275
  100.0 0.7 copy.12
  100.6 0.7 copy.13
  101.3 0.8 copy.16
  102.1 0.9 copy.17
  (1 shorter events, 0.0 us)
Async XLA Ops:
  0.6 0.8 copy-start.4
  1.4 0.7 copy-start.3
  2.1 1.0 %copy-start = (bf16[1,4,256,256]{3,2,1,0:T(8,128)(2,1)S(1)}, bf16[1,4,256,256]{3,2,1,0:T(8,128)(2,1)}, u32[]{:S(2)}) copy-start(bf16[1,4,256,256]{3,2,1,0:T(8,128)(2,1)} %x_ref.1) | copy-start | bytes 1572868
  3.1 1.0 %copy-start.1 = (bf16[4,256,256]{2,1,0:T(8,128)(2,1)S(1)}, bf16[4,256,256]{2,1,0:T(8,128)(2,1)}, u32[]{:S(2)}) copy-start(bf16[4,256,256]{2,1,0:T(8,128)(2,1)} %cot_ref.1) | copy-start | bytes 1572868
  4.2 1.0 copy-start.2

commit v2 on v1

v2 whole, which is shorter than its diff:
```python
import functools

import jax
import jax.numpy as jnp
from jax import lax
from jax.experimental import pallas as pl
from jax.experimental.pallas import tpu as pltpu
from jax.sharding import PartitionSpec as P

MESH = pl.DeviceIdType.MESH
F32 = jnp.float32
BF16 = jnp.bfloat16
HALO = 16
PARTS = 2


def rolled(value, shift):
    return pltpu.roll(value, shift % value.shape[0], 0)


def dot(left, right):
    return jnp.dot(left, right, preferred_element_type=F32)


def chain_body(sizes, x_ref, w_ref, gain_ref, shift_ref, bins_ref, cot_ref,
               din_ref, wgather, tiny_ref,
               xh, wv, wt, xt, gainv, shiftv, bins, hist, gown, dmat, dgrad, dpre, acc, small,
               wpart, wland, wsum, sland, ssum,
               load_s, hx_s, hx_r, hc_s, hc_r, wt_s, wt_r, d_s, d_r, ch_s, ch_r, pa_s, pa_r, pb_s, pb_r,
               z_s, z_r, zs_s, zs_r, y_s, y_r, ys_s, ys_r, ag_s, ag_r):
    sections, nz, ny, micro, rows, channels = sizes
    bulk = nz * ny
    ext = rows + 2 * HALO
    wide = 2 * HALO
    half = rows // 2
    unit = half + 2 * HALO
    blk = 3 * channels // nz
    cols = channels // PARTS
    own_count = micro // 2
    units = 2 * own_count
    s = lax.axis_index("section")
    b = lax.axis_index("bulk")
    c = lax.rem(s, 2)
    z = lax.rem(b, nz)
    y = b // nz
    peer = s + 1 - 2 * c
    left = lax.rem(b + bulk - 1, bulk)
    right = lax.rem(b + 1, bulk)
    first_chip = s >= sections - 2
    later_chip = s < sections - 2
    passes_on = s >= 2
    mine = own_count * c
    theirs = own_count * (1 - c)

    def z_peer(k):
        return y * nz + lax.rem(z + k, nz)

    def y_peer(k):
        return lax.rem(y + k, ny) * nz + z

    barrier = pltpu.get_barrier_semaphore()

    def greet(sec, blk_id):
        pl.semaphore_signal(barrier, inc=1, device_id=(sec, blk_id), device_id_type=MESH)

    greet(s, left)
    greet(s, right)
    greet(peer, b)

    @pl.when(passes_on)
    def _():
        greet(s - 2, b)

    @pl.when(later_chip)
    def _():
        greet(s + 2, b)

    for k in range(1, ny):
        greet(s, y_peer(k))
    for k in range(1, nz):
        greet(s, z_peer(k))

    def local(src, dst, k):
        return pltpu.make_async_copy(src, dst, load_s.at[k])

    loads = [
        local(w_ref.at[0], wv, 0),
        local(x_ref.at[0], xh.at[:, pl.ds(wide, rows)], 1),
        local(gain_ref, gainv, 2),
        local(shift_ref, shiftv, 3),
    ]
    for one in loads:
        one.start()
    cot_loads = [
        local(cot_ref.at[pl.ds(mine, own_count), pl.ds(0, unit - HALO)], hist.at[0, :, 0, pl.ds(HALO, unit - HALO)], 4),
        local(cot_ref.at[pl.ds(mine, own_count), pl.ds(rows - unit + HALO, unit - HALO)], hist.at[0, :, 1, pl.ds(0, unit - HALO)], 5),
    ]

    @pl.when(first_chip)
    def _():
        for one in cot_loads:
            one.start()

    for m in range(micro):
        bins[m] = bins_ref[m]
    loads[0].wait()
    for k in range(3):
        wt[c, k] = wv[k].astype(F32).T.astype(BF16)

    chain_peers = jnp.where(passes_on, 1, 0) + jnp.where(later_chip, 1, 0)
    pl.semaphore_wait(barrier, 3 + (nz - 1) + (ny - 1) + chain_peers)

    def copy(src, dst, send, recv, to):
        return pltpu.make_async_remote_copy(src_ref=src, dst_ref=dst, send_sem=send, recv_sem=recv, device_id=to, device_id_type=MESH)

    x_right = copy(x_ref.at[0, :, pl.ds(rows - wide, wide)], xh.at[:, pl.ds(0, wide)], hx_s.at[0], hx_r.at[0], (s, right))
    x_left = copy(x_ref.at[0, :, pl.ds(0, wide)], xh.at[:, pl.ds(wide + rows, wide)], hx_s.at[1], hx_r.at[1], (s, left))
    c_right = copy(cot_ref.at[pl.ds(mine, own_count), pl.ds(rows - HALO, HALO)], hist.at[0, :, 0, pl.ds(0, HALO)], hc_s.at[0], hc_r.at[0], (s, right))
    c_left = copy(cot_ref.at[pl.ds(mine, own_count), pl.ds(0, HALO)], hist.at[0, :, 1, pl.ds(unit - HALO, HALO)], hc_s.at[1], hc_r.at[1], (s, left))
    w_peer = copy(wt.at[c], wt.at[c], wt_s.at[0], wt_r.at[0], (peer, b))
    x_right.start()
    x_left.start()

    @pl.when(first_chip)
    def _():
        c_right.start()
        c_left.start()

    w_peer.start()
    for one in loads[1:]:
        one.wait()
    x_right.wait_recv()
    x_left.wait_recv()

    def d_copy(j):
        m = theirs + j
        return copy(dmat.at[c, m], dmat.at[c, m], d_s.at[j], d_r.at[j], (peer, b))

    def forward(j, carry):
        m = lax.rem(theirs + j, micro)
        xs = xh[m]
        pre = rolled(dot(xs, wv[0]), 1) + dot(xs, wv[1]) + rolled(dot(xs, wv[2]), -1)
        pre = pre[HALO:HALO + ext]
        k = bins[m]
        gain = gainv[k]
        filmed = pre * gain + shiftv[k]
        sig = jax.nn.sigmoid(filmed)
        d = sig * (1.0 + filmed * (1.0 - sig))
        dmat[c, m] = d * gain

        @pl.when(j < own_count)
        def _():
            d_copy(j).start()

        d = d[HALO:HALO + rows]
        dgrad[m] = d
        dpre[m] = d * pre[HALO:HALO + rows]
        return carry

    lax.fori_loop(0, micro, forward, 0)

    def turn(m, carry):
        xs = xh[m].astype(F32)
        for j, sh in enumerate((1, 0, -1)):
            part = rolled(xs, sh) if sh else xs
            xt[m, j * channels:(j + 1) * channels] = part[wide:wide + rows].T.astype(BF16)
        return carry

    acc[...] = jnp.zeros_like(acc)

    def weight_step(m):
        g = gown[m].astype(F32)
        gp = (g * dmat[c, m, HALO:HALO + rows]).astype(BF16)
        acc[...] += dot(xt[m], gp)
        small[pl.ds(m, 1)] = jnp.sum(g * dpre[m], 0, keepdims=True)
        small[pl.ds(micro + m, 1)] = jnp.sum(g * dgrad[m], 0, keepdims=True)

    @pl.when(later_chip)
    def _():
        lax.fori_loop(0, micro, turn, 0)

    @pl.when(first_chip)
    def _():
        for one in cot_loads:
            one.wait()
        c_right.wait_recv()
        c_left.wait_recv()

    w_peer.wait_recv()

    def split(u):
        i = u // 2
        return i, u - 2 * i

    def chain_copy(u):
        i, h = split(u)
        return copy(hist.at[2, i, h], hist.at[0, i, h], ch_s.at[u], ch_r.at[u], (s - 2, b))

    def spot_of(u):
        i, h = split(u)
        return mine + i, pl.ds(pl.multiple_of(h * half, half), half)

    def grad_copy(u):
        i, h = split(u)
        m, at = spot_of(u)
        return copy(hist.at[c, i, h, pl.ds(HALO, half)], gown.at[m, at], pa_s.at[u], pa_r.at[u], (peer, b))

    def out_copy(u):
        i, h = split(u)
        m, at = spot_of(u)
        return copy(hist.at[c + 1, i, h, pl.ds(HALO, half)], din_ref.at[m, at], pb_s.at[u], pb_r.at[u], (peer, b))

    def back(g, sec, m, at):
        gp = (g * dmat[sec, m, at]).astype(BF16)
        out = g + dot(gp, wt[sec, 1])
        out = out + rolled(dot(gp, wt[sec, 0]), -1)
        out = out + rolled(dot(gp, wt[sec, 2]), 1)
        return out.astype(BF16)

    def chain(u, carry):
        i, h = split(u)
        m, at = spot_of(u)
        span = pl.ds(pl.multiple_of(h * half, half), unit)

        @pl.when(h == 0)
        def _():
            d_copy(i).wait_recv()

        @pl.when(later_chip)
        def _():
            chain_copy(u).wait_recv()

        upper = back(hist[0, i, h].astype(F32), 1, m, span)
        hist[1, i, h] = upper
        lower = back(upper.astype(F32), 0, m, span)
        hist[2, i, h] = lower

        @pl.when(passes_on)
        def _():
            chain_copy(u).start()

        grad_copy(u).start()
        out_copy(u).start()
        gown[m, at] = hist[1 - c, i, h, HALO:HALO + half]
        din_ref[m, at] = hist[2 - c, i, h, HALO:HALO + half]

        @pl.when(later_chip & (h == 1))
        def _():
            weight_step(m)

        @pl.when(later_chip & (h == 0) & (i > 0))
        def _():
            grad_copy(u - 2).wait_recv()
            grad_copy(u - 1).wait_recv()
            weight_step(theirs + i - 1)

        return carry

    lax.fori_loop(0, units, chain, 0)

    @pl.when(first_chip)
    def _():
        lax.fori_loop(0, micro, turn, 0)
        for i in range(own_count):
            weight_step(mine + i)
        for i in range(own_count - 1):
            grad_copy(2 * i).wait_recv()
            grad_copy(2 * i + 1).wait_recv()
            weight_step(theirs + i)

    grad_copy(units - 2).wait_recv()
    grad_copy(units - 1).wait_recv()
    weight_step(theirs + own_count - 1)

    def scatter(q, k):
        to = lax.rem(z + k, nz)
        return copy(wpart.at[q, to], wland.at[q, k], z_s.at[q, k], z_r.at[q, k], (s, y * nz + to))

    def small_z(k):
        return copy(small, sland.at[k], zs_s.at[k], zs_r.at[k], (s, z_peer(k)))

    def across(q, k):
        return copy(wsum.at[q, y], wsum.at[q, y], y_s.at[q, k], y_r.at[q, k], (s, y_peer(k)))

    def small_y(k):
        return copy(ssum.at[y], ssum.at[y], ys_s.at[k], ys_r.at[k], (s, y_peer(k)))

    def gather(q, k):
        return copy(wgather.at[q, z], wgather.at[q, z], ag_s.at[q, k], ag_r.at[q, k], (s, z_peer(k)))

    for q in range(PARTS):
        for j in range(nz):
            wpart[q, j] = acc[j * blk:(j + 1) * blk, q * cols:(q + 1) * cols].astype(BF16)
        for k in range(1, nz):
            scatter(q, k).start()
    for k in range(1, nz):
        small_z(k).start()

    for q in range(PARTS):
        total = wpart[q, z].astype(F32)
        for k in range(1, nz):
            scatter(q, k).wait_recv()
            total = total + wland[q, k].astype(F32)
        wsum[q, y] = total.astype(BF16)
        for k in range(1, ny):
            across(q, k).start()

    sland[0] = small[...]
    for k in range(1, nz):
        small_z(k).wait_recv()
    tiny = sland[z]
    for j in range(1, nz):
        tiny = tiny + sland[lax.rem(z + nz - j, nz)]
    ssum[y] = tiny
    for k in range(1, ny):
        small_y(k).start()

    for q in range(PARTS):
        for k in range(1, ny):
            across(q, k).wait_recv()
        total = wsum[q, 0].astype(F32)
        for j in range(1, ny):
            total = total + wsum[q, j].astype(F32)
        wgather[q, z] = total.astype(BF16)
        for k in range(1, nz):
            gather(q, k).start()

    for k in range(1, ny):
        small_y(k).wait_recv()
    tiny = ssum[0]
    for j in range(1, ny):
        tiny = tiny + ssum[j]
    tiny_ref[...] = tiny

    x_right.wait_send()
    x_left.wait_send()
    w_peer.wait_send()

    @pl.when(first_chip)
    def _():
        c_right.wait_send()
        c_left.wait_send()

    for j in range(own_count):
        d_copy(j).wait_send()
    for u in range(units):
        grad_copy(u).wait_send()
        out_copy(u).wait()

    @pl.when(passes_on)
    def _():
        for u in range(units):
            chain_copy(u).wait_send()

    for k in range(1, nz):
        small_z(k).wait_send()
    for k in range(1, ny):
        small_y(k).wait_send()
    for q in range(PARTS):
        for k in range(1, nz):
            scatter(q, k).wait_send()
        for k in range(1, ny):
            across(q, k).wait_send()
        for k in range(1, nz):
            gather(q, k).wait()


def finish_body(din_ref, wgather, tiny_ref, bins_ref, din_out, dw_out, gain_out, shift_out, wide_w, gains, shifts, sems):
    parts, nz, blk, cols = wgather.shape
    micro = tiny_ref.shape[0] // 2
    channels = cols * parts
    copies = [pltpu.make_async_copy(din_ref, din_out.at[0], sems.at[0])]
    copies[0].start()
    for j in range(nz):
        for q in range(parts):
            wide_w[j * blk:(j + 1) * blk, q * cols:(q + 1) * cols] = wgather[q, j].astype(F32)
    copies.append(pltpu.make_async_copy(wide_w, dw_out.at[0], sems.at[1]))
    copies[1].start()
    count = gains.shape[0]
    spot = lax.broadcasted_iota(jnp.int32, (count, 1, channels), 0)
    out_gain = jnp.zeros((count, 1, channels), F32)
    out_shift = jnp.zeros((count, 1, channels), F32)
    for m in range(micro):
        hit = spot == bins_ref[m]
        out_gain = out_gain + jnp.where(hit, tiny_ref[m:m + 1][None], 0.0)
        out_shift = out_shift + jnp.where(hit, tiny_ref[micro + m:micro + m + 1][None], 0.0)
    gains[...] = out_gain
    shifts[...] = out_shift
    copies.append(pltpu.make_async_copy(gains, gain_out, sems.at[2]))
    copies.append(pltpu.make_async_copy(shifts, shift_out, sems.at[3]))
    copies[2].start()
    copies[3].start()
    for one in copies:
        one.wait()


def shards(sections, bulk, activations, weights, film_gain, film_shift, doa_bins, cotangent):
    micro, rows, channels = activations.shape[1:]
    bins_count = film_gain.shape[1]
    nz = 8 if bulk == 32 else 2
    ny = bulk // nz
    ext = rows + 2 * HALO
    blk = 3 * channels // nz
    cols = channels // PARTS
    own = micro // 2
    unit = rows // 2 + 2 * HALO
    sizes = (sections, nz, ny, micro, rows, channels)
    dma = pltpu.SemaphoreType.DMA
    vmem = pl.BlockSpec(memory_space=pltpu.VMEM)
    hbm = pl.BlockSpec(memory_space=pltpu.HBM)
    smem = pl.BlockSpec(memory_space=pltpu.SMEM)
    scratch = pltpu.VMEM
    gain_rows = jnp.transpose(film_gain, (1, 0, 2))
    shift_rows = jnp.transpose(film_shift, (1, 0, 2))
    d_in, w_sum, tiny = pl.pallas_call(
        functools.partial(chain_body, sizes),
        out_shape=(
            jax.ShapeDtypeStruct((micro, rows, channels), BF16),
            jax.ShapeDtypeStruct((PARTS, nz, blk, cols), BF16),
            jax.ShapeDtypeStruct((2 * micro, channels), F32),
        ),
        in_specs=[hbm, hbm, hbm, hbm, smem, hbm],
        out_specs=(vmem, vmem, vmem),
        scratch_shapes=[
            scratch((micro, ext + 2 * HALO, channels), BF16),
            scratch((3, channels, channels), BF16),
            scratch((2, 3, channels, channels), BF16),
            scratch((micro, 3 * channels, rows), BF16),
            scratch((bins_count, 1, channels), F32),
            scratch((bins_count, 1, channels), F32),
            pltpu.SMEM((micro,), jnp.int32),
            scratch((3, own, 2, unit, channels), BF16),
            scratch((micro, rows, channels), BF16),
            scratch((2, micro, ext, channels), F32),
            scratch((micro, rows, channels), F32),
            scratch((micro, rows, channels), F32),
            scratch((3 * channels, channels), F32),
            scratch((2 * micro, channels), F32),
            scratch((PARTS, nz, blk, cols), BF16),
            scratch((PARTS, nz, blk, cols), BF16),
            scratch((PARTS, ny, blk, cols), BF16),
            scratch((nz, 2 * micro, channels), F32),
            scratch((ny, 2 * micro, channels), F32),
            dma((6,)), dma((2,)), dma((2,)), dma((2,)), dma((2,)), dma((1,)), dma((1,)),
            dma((own,)), dma((own,)), dma((2 * own,)), dma((2 * own,)),
            dma((2 * own,)), dma((2 * own,)), dma((2 * own,)), dma((2 * own,)),
            dma((PARTS, nz)), dma((PARTS, nz)), dma((nz,)), dma((nz,)),
            dma((PARTS, ny)), dma((PARTS, ny)), dma((ny,)), dma((ny,)),
            dma((PARTS, nz)), dma((PARTS, nz)),
        ],
        compiler_params=pltpu.CompilerParams(
            collective_id=0, has_side_effects=True, vmem_limit_bytes=48 * 1024 * 1024
        ),
    )(activations, weights, gain_rows, shift_rows, doa_bins, cotangent)
    d_in, d_w, d_gain, d_shift = pl.pallas_call(
        finish_body,
        out_shape=(
            jax.ShapeDtypeStruct((1, micro, rows, channels), BF16),
            jax.ShapeDtypeStruct((1, 3 * channels, channels), F32),
            jax.ShapeDtypeStruct((bins_count, 1, channels), F32),
            jax.ShapeDtypeStruct((bins_count, 1, channels), F32),
        ),
        in_specs=[vmem, vmem, vmem, smem],
        out_specs=(hbm, hbm, hbm, hbm),
        scratch_shapes=[
            scratch((3 * channels, channels), F32),
            scratch((bins_count, 1, channels), F32),
            scratch((bins_count, 1, channels), F32),
            dma((4,)),
        ],
        compiler_params=pltpu.CompilerParams(vmem_limit_bytes=16 * 1024 * 1024),
    )(d_in, w_sum, tiny, doa_bins)
    return (
        d_in,
        d_w.reshape(1, 3, channels, channels),
        jnp.transpose(d_gain, (1, 0, 2)),
        jnp.transpose(d_shift, (1, 0, 2)),
    )


def solution(mesh):
    return jax.shard_map(
        functools.partial(shards, mesh.shape["section"], mesh.shape["bulk"]),
        mesh=mesh,
        in_specs=(
            P("section", None, "bulk", None),
            P("section", None, None, None),
            P("section", None, None),
            P("section", None, None),
            P(),
            P(None, "bulk", None),
        ),
        out_specs=(
            P("section", None, "bulk", None),
            P("section", None, None, None),
            P("section", None, None),
            P("section", None, None),
        ),
        check_vma=False,
    )
```

time: 104 us -> 95.9 us (0.922)
  Pallas kernels: 94.8 us -> 89.6 us
  local copies, waits for them, and re-layouts: 7.49 us -> 5.26 us
    pallas_call x1 -> x2, Pallas kernels: 94.8 us -> 89.6 us  [the longest x1 88 us: shards(): pl.pallas_call(functools.partial(chain_body, sizes), out_shape=(jax.Shape...]
    unnamed x16 -> x12, local copies, waits for them, and re-layouts: 7.49 us -> 5.26 us
where the time goes in v2:
time: 95.9 us; the launch traced here: 95.5 us
  Pallas kernels  89.6 us (93%)
  local copies, waits for them, and re-layouts  5.26 us (5%)
    pallas_call x1, Pallas kernels, shards(): pl.pallas_call(functools.partial(chain_body, sizes), out_shape=(jax.Shape...  88 us
    unnamed x12, local copies, waits for them, and re-layouts  5.26 us

profile of v2, /device:TPU:1, one launch (start us, length us, event | category | flops | bytes accessed | tf_op | source)
XLA Modules:
  0.0 95.5 jit_solution(3143310780982088853)
XLA Ops:
  0.6 0.0 copy-start.5
  0.6 0.6 copy-done.5
  1.3 0.0 copy-start
  1.3 1.0 %copy-done = bf16[1,4,256,256]{3,2,1,0:T(8,128)(2,1)S(1)} copy-done((bf16[1,4,256,256]{3,2,1,0:T(8,128)(2,1)S(1)}, bf16[1,4,256,256]{3,2,1,0:T(8,128)(2,1)}, u32[]{:S(2)}) %copy-start) | copy-done | bytes 524312
  2.3 0.0 copy-start.1
  2.3 1.0 %copy-done.1 = bf16[4,256,256]{2,1,0:T(8,128)(2,1)S(1)} copy-done((bf16[4,256,256]{2,1,0:T(8,128)(2,1)S(1)}, bf16[4,256,256]{2,1,0:T(8,128)(2,1)}, u32[]{:S(2)}) %copy-start.1) | copy-done | bytes 524312
  3.4 0.0 copy-start.2
  3.4 1.0 %copy-done.2 = bf16[1,3,256,256]{3,2,1,0:T(8,128)(2,1)S(1)} copy-done((bf16[1,3,256,256]{3,2,1,0:T(8,128)(2,1)S(1)}, bf16[1,3,256,256]{3,2,1,0:T(8,128)(2,1)}, u32[]{:S(2)}) %copy-start.2) | copy-done | bytes 393240
  4.4 0.0 copy-start.3
  4.4 0.8 copy-done.3
  5.1 0.0 copy-start.4
  5.1 0.8 copy-done.4
  5.9 88.0 %shard_map.93 = (bf16[4,256,256]{2,1,0:T(8,128)(2,1)S(1)}, bf16[2,8,96,128]{3,2,1,0:T(8,128)(2,1)S(1)}, f32[8,256]{1,0:T(8,128)S(1)}) custom-call(bf16[1,4,256,256]{3,2,1,0:T(8,128)(2,1)S(1)} %copy-done, bf16[1,3,256,256]{3,2,1,0:T(8,128)(2,1)S(1)} %copy-done.2, f32[36,1,256]{2,1,0:T(1,128)S(1)} %bitcast.5, f32[36,1,256]{2,1,0:T(1,128)S(1)} %bitcast.6, ...), custom_call_target="tpu_custom_call" | custom-call | tf_op jit(solution)/shard_map/pallas_call | solution.py:415
  93.9 1.6 %shard_map.94 = (bf16[1,4,256,256]{3,2,1,0:T(8,128)(2,1)}, f32[1,768,256]{2,1,0:T(8,128)}, f32[36,1,256]{2,1,0:T(1,128)}, f32[36,1,256]{2,1,0:T(1,128)}) custom-call(bf16[4,256,256]{2,1,0:T(8,128)(2,1)S(1)} %get-tuple-element.11.din_ref, bf16[2,8,96,128]{3,2,1,0:T(8,128)(2,1)S(1)} %get-tuple-element.12.wgather, f32[8,256]{1,0:T(8,128)S(1)} %get-tuple-element.13.tiny_ref, ...), custom_call_target="tpu_custom_call" | custom-call | tf_op jit(solution)/shard_map/pallas_call | solution.py:455
Async XLA Ops:
  0.6 0.7 copy-start.5
  1.3 1.0 %copy-start = (bf16[1,4,256,256]{3,2,1,0:T(8,128)(2,1)S(1)}, bf16[1,4,256,256]{3,2,1,0:T(8,128)(2,1)}, u32[]{:S(2)}) copy-start(bf16[1,4,256,256]{3,2,1,0:T(8,128)(2,1)} %x_ref.1) | copy-start | bytes 1572868
  2.3 1.0 %copy-start.1 = (bf16[4,256,256]{2,1,0:T(8,128)(2,1)S(1)}, bf16[4,256,256]{2,1,0:T(8,128)(2,1)}, u32[]{:S(2)}) copy-start(bf16[4,256,256]{2,1,0:T(8,128)(2,1)} %cot_ref.1) | copy-start | bytes 1572868
  3.4 1.0 %copy-start.2 = (bf16[1,3,256,256]{3,2,1,0:T(8,128)(2,1)S(1)}, bf16[1,3,256,256]{3,2,1,0:T(8,128)(2,1)}, u32[]{:S(2)}) copy-start(bf16[1,3,256,256]{3,2,1,0:T(8,128)(2,1)} %w_ref.1) | copy-start | bytes 1179652
  4.4 0.8 copy-start.3
  5.1 0.8 copy-start.4

commit v3 on v2

--- a/solution.py
+++ b/solution.py
@@ -11,7 +11,10 @@
 F32 = jnp.float32
 BF16 = jnp.bfloat16
 HALO = 16
-PARTS = 2
+ROW_PARTS = 2
+COL_PARTS = 2
+PARTS = ROW_PARTS * COL_PARTS
+SPLIT = 4
 
 
 def rolled(value, shift):
@@ -23,21 +26,24 @@
 
 
 def chain_body(sizes, x_ref, w_ref, gain_ref, shift_ref, bins_ref, cot_ref,
-               din_ref, wgather, tiny_ref,
+               din_ref, dw_ref, gain_out, shift_out,
                xh, wv, wt, xt, gainv, shiftv, bins, hist, gown, dmat, dgrad, dpre, acc, small,
-               wpart, wland, wsum, sland, ssum,
-               load_s, hx_s, hx_r, hc_s, hc_r, wt_s, wt_r, d_s, d_r, ch_s, ch_r, pa_s, pa_r, pb_s, pb_r,
+               wpart, wland, wsum, wgather, wide_w, gains, shifts, sland, ssum,
+               load_s, own_s, store_s, hx_s, hx_r, hc_s, hc_r, wt_s, wt_r, d_s, d_r, ch_s, ch_r, pa_s, pa_r, pb_s, pb_r,
                z_s, z_r, zs_s, zs_r, y_s, y_r, ys_s, ys_r, ag_s, ag_r):
     sections, nz, ny, micro, rows, channels = sizes
     bulk = nz * ny
     ext = rows + 2 * HALO
     wide = 2 * HALO
-    half = rows // 2
+    half = rows // SPLIT
     unit = half + 2 * HALO
     blk = 3 * channels // nz
-    cols = channels // PARTS
+    sub = blk // ROW_PARTS
+    cols = channels // COL_PARTS
     own_count = micro // 2
-    units = 2 * own_count
+    units = SPLIT * own_count
+    z_order = sorted(range(1, nz), key=lambda k: -min(k, nz - k))
+    y_order = sorted(range(1, ny), key=lambda k: -min(k, ny - k))
     s = lax.axis_index("section")
     b = lax.axis_index("bulk")
     c = lax.rem(s, 2)
@@ -91,10 +97,13 @@
     ]
     for one in loads:
         one.start()
-    cot_loads = [
-        local(cot_ref.at[pl.ds(mine, own_count), pl.ds(0, unit - HALO)], hist.at[0, :, 0, pl.ds(HALO, unit - HALO)], 4),
-        local(cot_ref.at[pl.ds(mine, own_count), pl.ds(rows - unit + HALO, unit - HALO)], hist.at[0, :, 1, pl.ds(0, unit - HALO)], 5),
-    ]
+    cot_loads = []
+    for h in range(SPLIT):
+        start = max(0, half * h - HALO)
+        count = min(rows, half * h + half + HALO) - start
+        cot_loads.append(local(
+            cot_ref.at[pl.ds(mine, own_count), pl.ds(start, count)],
+            hist.at[0, :, h, pl.ds(start - half * h + HALO, count)], 4 + h))
 
     @pl.when(first_chip)
     def _():
@@ -116,7 +125,7 @@
     x_right = copy(x_ref.at[0, :, pl.ds(rows - wide, wide)], xh.at[:, pl.ds(0, wide)], hx_s.at[0], hx_r.at[0], (s, right))
     x_left = copy(x_ref.at[0, :, pl.ds(0, wide)], xh.at[:, pl.ds(wide + rows, wide)], hx_s.at[1], hx_r.at[1], (s, left))
     c_right = copy(cot_ref.at[pl.ds(mine, own_count), pl.ds(rows - HALO, HALO)], hist.at[0, :, 0, pl.ds(0, HALO)], hc_s.at[0], hc_r.at[0], (s, right))
-    c_left = copy(cot_ref.at[pl.ds(mine, own_count), pl.ds(0, HALO)], hist.at[0, :, 1, pl.ds(unit - HALO, HALO)], hc_s.at[1], hc_r.at[1], (s, left))
+    c_left = copy(cot_ref.at[pl.ds(mine, own_count), pl.ds(0, HALO)], hist.at[0, :, SPLIT - 1, pl.ds(unit - HALO, HALO)], hc_s.at[1], hc_r.at[1], (s, left))
     w_peer = copy(wt.at[c], wt.at[c], wt_s.at[0], wt_r.at[0], (peer, b))
     x_right.start()
     x_left.start()
@@ -129,32 +138,52 @@
     w_peer.start()
     for one in loads[1:]:
         one.wait()
-    x_right.wait_recv()
-    x_left.wait_recv()
-
-    def d_copy(j):
-        m = theirs + j
-        return copy(dmat.at[c, m], dmat.at[c, m], d_s.at[j], d_r.at[j], (peer, b))
-
-    def forward(j, carry):
-        m = lax.rem(theirs + j, micro)
-        xs = xh[m]
-        pre = rolled(dot(xs, wv[0]), 1) + dot(xs, wv[1]) + rolled(dot(xs, wv[2]), -1)
-        pre = pre[HALO:HALO + ext]
-        k = bins[m]
+
+    def taps(xs):
+        return rolled(dot(xs, wv[0]), 1) + dot(xs, wv[1]) + rolled(dot(xs, wv[2]), -1)
+
+    def film(pre, k):
         gain = gainv[k]
         filmed = pre * gain + shiftv[k]
         sig = jax.nn.sigmoid(filmed)
         d = sig * (1.0 + filmed * (1.0 - sig))
-        dmat[c, m] = d * gain
+        return d, d * gain
+
+    def inner(m, carry):
+        pre = taps(xh[m, wide:wide + rows])
+        d, full = film(pre, bins[m])
+        dmat[c, m, HALO:HALO + rows] = full
+        dgrad[m] = d
+        dpre[m] = d * pre
+        return carry
+
+    lax.fori_loop(0, micro, inner, 0)
+    x_right.wait_recv()
+    x_left.wait_recv()
+
+    def d_copy(j):
+        m = theirs + j
+        return copy(dmat.at[c, m], dmat.at[c, m], d_s.at[j], d_r.at[j], (peer, b))
+
+    def forward(j, carry):
+        m = lax.rem(theirs + j, micro)
+        ends = jnp.concatenate([xh[m, 0:2 * wide], xh[m, rows:rows + 2 * wide]], axis=0)
+        pre = taps(ends)
+        d, full = film(pre, bins[m])
+        low = slice(HALO, HALO + wide)
+        high = slice(2 * wide + HALO, 3 * wide + HALO)
+        dmat[c, m, 0:wide] = full[low]
+        dmat[c, m, rows:rows + wide] = full[high]
 
         @pl.when(j < own_count)
         def _():
             d_copy(j).start()
 
-        d = d[HALO:HALO + rows]
-        dgrad[m] = d
-        dpre[m] = d * pre[HALO:HALO + rows]
+        both = d * pre
+        dgrad[m, 0:HALO] = d[wide:wide + HALO]
+        dpre[m, 0:HALO] = both[wide:wide + HALO]
+        dgrad[m, rows - HALO:rows] = d[high][0:HALO]
+        dpre[m, rows - HALO:rows] = both[high][0:HALO]
         return carry
 
     lax.fori_loop(0, micro, forward, 0)
@@ -189,8 +218,8 @@
     w_peer.wait_recv()
 
     def split(u):
-        i = u // 2
-        return i, u - 2 * i
+        i = u // SPLIT
+        return i, u - SPLIT * i
 
     def chain_copy(u):
         i, h = split(u)
@@ -209,6 +238,11 @@
         i, h = split(u)
         m, at = spot_of(u)
         return copy(hist.at[c + 1, i, h, pl.ds(HALO, half)], din_ref.at[m, at], pb_s.at[u], pb_r.at[u], (peer, b))
+
+    def own_copy(u):
+        i, h = split(u)
+        m, at = spot_of(u)
+        return pltpu.make_async_copy(hist.at[2 - c, i, h, pl.ds(HALO, half)], din_ref.at[m, at], own_s.at[u])
 
     def back(g, sec, m, at):
         gp = (g * dmat[sec, m, at]).astype(BF16)
@@ -241,17 +275,17 @@
 
         grad_copy(u).start()
         out_copy(u).start()
+        own_copy(u).start()
         gown[m, at] = hist[1 - c, i, h, HALO:HALO + half]
-        din_ref[m, at] = hist[2 - c, i, h, HALO:HALO + half]
-
-        @pl.when(later_chip & (h == 1))
+
+        @pl.when(later_chip & (h == SPLIT - 1))
         def _():
             weight_step(m)
 
         @pl.when(later_chip & (h == 0) & (i > 0))
         def _():
-            grad_copy(u - 2).wait_recv()
-            grad_copy(u - 1).wait_recv()
+            for k in range(SPLIT):
+                grad_copy(u - SPLIT + k).wait_recv()
             weight_step(theirs + i - 1)
 
         return carry
@@ -264,12 +298,12 @@
         for i in range(own_count):
             weight_step(mine + i)
         for i in range(own_count - 1):
-            grad_copy(2 * i).wait_recv()
-            grad_copy(2 * i + 1).wait_recv()
+            for k in range(SPLIT):
+                grad_copy(SPLIT * i + k).wait_recv()
             weight_step(theirs + i)
 
-    grad_copy(units - 2).wait_recv()
-    grad_copy(units - 1).wait_recv()
+    for k in range(SPLIT):
+        grad_copy(units - SPLIT + k).wait_recv()
     weight_step(theirs + own_count - 1)
 
     def scatter(q, k):
@@ -288,21 +322,26 @@
     def gather(q, k):
         return copy(wgather.at[q, z], wgather.at[q, z], ag_s.at[q, k], ag_r.at[q, k], (s, z_peer(k)))
 
+    def area(q, j):
+        top, side = j * blk + (q // COL_PARTS) * sub, (q % COL_PARTS) * cols
+        return slice(top, top + sub), slice(side, side + cols)
+
     for q in range(PARTS):
         for j in range(nz):
-            wpart[q, j] = acc[j * blk:(j + 1) * blk, q * cols:(q + 1) * cols].astype(BF16)
-        for k in range(1, nz):
+            at_rows, at_cols = area(q, j)
+            wpart[q, j] = acc[at_rows, at_cols].astype(BF16)
+        for k in z_order:
             scatter(q, k).start()
-    for k in range(1, nz):
+    for k in z_order:
         small_z(k).start()
 
     for q in range(PARTS):
         total = wpart[q, z].astype(F32)
-        for k in range(1, nz):
+        for k in z_order:
             scatter(q, k).wait_recv()
             total = total + wland[q, k].astype(F32)
         wsum[q, y] = total.astype(BF16)
-        for k in range(1, ny):
+        for k in y_order:
             across(q, k).start()
 
     sland[0] = small[...]
@@ -312,7 +351,7 @@
     for j in range(1, nz):
         tiny = tiny + sland[lax.rem(z + nz - j, nz)]
     ssum[y] = tiny
-    for k in range(1, ny):
+    for k in y_order:
         small_y(k).start()
 
     for q in range(PARTS):
@@ -322,7 +361,7 @@
         for j in range(1, ny):
             total = total + wsum[q, j].astype(F32)
         wgather[q, z] = total.astype(BF16)
-        for k in range(1, nz):
+        for k in z_order:
             gather(q, k).start()
 
     for k in range(1, ny):
@@ -330,7 +369,22 @@
     tiny = ssum[0]
     for j in range(1, ny):
         tiny = tiny + ssum[j]
-    tiny_ref[...] = tiny
+    count = gains.shape[0]
+    spot = lax.broadcasted_iota(jnp.int32, (count, 1, channels), 0)
+    sum_gain = jnp.zeros((count, 1, channels), F32)
+    sum_shift = jnp.zeros((count, 1, channels), F32)
+    for m in range(micro):
+        hit = spot == bins[m]
+        sum_gain = sum_gain + jnp.where(hit, tiny[m:m + 1][None], 0.0)
+        sum_shift = sum_shift + jnp.where(hit, tiny[micro + m:micro + m + 1][None], 0.0)
+    gains[...] = sum_gain
+    shifts[...] = sum_shift
+    stores = [
+        pltpu.make_async_copy(gains, gain_out, store_s.at[0]),
+        pltpu.make_async_copy(shifts, shift_out, store_s.at[1]),
+    ]
+    for one in stores:
+        one.start()
 
     x_right.wait_send()
     x_left.wait_send()
@@ -346,6 +400,7 @@
     for u in range(units):
         grad_copy(u).wait_send()
         out_copy(u).wait()
+        own_copy(u).wait()
 
     @pl.when(passes_on)
     def _():
@@ -358,40 +413,36 @@
         small_y(k).wait_send()
     for q in range(PARTS):
         for k in range(1, nz):
+            gather(q, k).wait()
+        for j in range(nz):
+            at_rows, at_cols = area(q, j)
+            wide_w[at_rows, at_cols] = wgather[q, j].astype(F32)
+    stores.append(pltpu.make_async_copy(wide_w, dw_ref, store_s.at[2]))
+    stores[2].start()
+    for one in stores:
+        one.wait()
+    for q in range(PARTS):
+        for k in range(1, nz):
             scatter(q, k).wait_send()
         for k in range(1, ny):
             across(q, k).wait_send()
-        for k in range(1, nz):
-            gather(q, k).wait()
-
-
-def finish_body(din_ref, wgather, tiny_ref, bins_ref, din_out, dw_out, gain_out, shift_out, wide_w, gains, shifts, sems):
-    parts, nz, blk, cols = wgather.shape
-    micro = tiny_ref.shape[0] // 2
-    channels = cols * parts
-    copies = [pltpu.make_async_copy(din_ref, din_out.at[0], sems.at[0])]
-    copies[0].start()
-    for j in range(nz):
-        for q in range(parts):
-            wide_w[j * blk:(j + 1) * blk, q * cols:(q + 1) * cols] = wgather[q, j].astype(F32)
-    copies.append(pltpu.make_async_copy(wide_w, dw_out.at[0], sems.at[1]))
-    copies[1].start()
-    count = gains.shape[0]
-    spot = lax.broadcasted_iota(jnp.int32, (count, 1, channels), 0)
-    out_gain = jnp.zeros((count, 1, channels), F32)
-    out_shift = jnp.zeros((count, 1, channels), F32)
-    for m in range(micro):
-        hit = spot == bins_ref[m]
-        out_gain = out_gain + jnp.where(hit, tiny_ref[m:m + 1][None], 0.0)
-        out_shift = out_shift + jnp.where(hit, tiny_ref[micro + m:micro + m + 1][None], 0.0)
-    gains[...] = out_gain
-    shifts[...] = out_shift
-    copies.append(pltpu.make_async_copy(gains, gain_out, sems.at[2]))
-    copies.append(pltpu.make_async_copy(shifts, shift_out, sems.at[3]))
-    copies[2].start()
-    copies[3].start()
-    for one in copies:
+
+
+def finish_body(din_ref, dw_ref, gain_ref, shift_ref, din_out, dw_out, gain_out, shift_out, din, dw, gains, shifts, load_s, store_s):
+    micro = din_ref.shape[0]
+    tap = dw_ref.shape[0] // 3
+    trips = [(dw_ref.at[pl.ds(k * tap, tap)], dw.at[k], dw_out.at[0, k]) for k in range(3)]
+    trips += [(din_ref.at[m], din.at[m], din_out.at[0, m]) for m in range(micro)]
+    trips += [(gain_ref, gains, gain_out), (shift_ref, shifts, shift_out)]
+    loads = [pltpu.make_async_copy(src, mid, load_s.at[k]) for k, (src, mid, _) in enumerate(trips)]
+    stores = [pltpu.make_async_copy(mid, dst, store_s.at[k]) for k, (_, mid, dst) in enumerate(trips)]
+    for one in loads:
+        one.start()
+    for one, two in zip(loads, stores):
         one.wait()
+        two.start()
+    for two in stores:
+        two.wait()
 
 
 def shards(sections, bulk, activations, weights, film_gain, film_shift, doa_bins, cotangent):
@@ -401,26 +452,28 @@
     ny = bulk // nz
     ext = rows + 2 * HALO
     blk = 3 * channels // nz
-    cols = channels // PARTS
+    sub = blk // ROW_PARTS
+    cols = channels // COL_PARTS
     own = micro // 2
-    unit = rows // 2 + 2 * HALO
+    units = SPLIT * own
+    unit = rows // SPLIT + 2 * HALO
     sizes = (sections, nz, ny, micro, rows, channels)
     dma = pltpu.SemaphoreType.DMA
-    vmem = pl.BlockSpec(memory_space=pltpu.VMEM)
     hbm = pl.BlockSpec(memory_space=pltpu.HBM)
     smem = pl.BlockSpec(memory_space=pltpu.SMEM)
     scratch = pltpu.VMEM
     gain_rows = jnp.transpose(film_gain, (1, 0, 2))
     shift_rows = jnp.transpose(film_shift, (1, 0, 2))
-    d_in, w_sum, tiny = pl.pallas_call(
+    held = pl.pallas_call(
         functools.partial(chain_body, sizes),
         out_shape=(
             jax.ShapeDtypeStruct((micro, rows, channels), BF16),
-            jax.ShapeDtypeStruct((PARTS, nz, blk, cols), BF16),
-            jax.ShapeDtypeStruct((2 * micro, channels), F32),
+            jax.ShapeDtypeStruct((3 * channels, channels), F32),
+            jax.ShapeDtypeStruct((bins_count, 1, channels), F32),
+            jax.ShapeDtypeStruct((bins_count, 1, channels), F32),
         ),
         in_specs=[hbm, hbm, hbm, hbm, smem, hbm],
-        out_specs=(vmem, vmem, vmem),
+        out_specs=(hbm, hbm, hbm, hbm),
         scratch_shapes=[
             scratch((micro, ext + 2 * HALO, channels), BF16),
             scratch((3, channels, channels), BF16),
@@ -429,50 +482,57 @@
             scratch((bins_count, 1, channels), F32),
             scratch((bins_count, 1, channels), F32),
             pltpu.SMEM((micro,), jnp.int32),
-            scratch((3, own, 2, unit, channels), BF16),
+            scratch((3, own, SPLIT, unit, channels), BF16),
             scratch((micro, rows, channels), BF16),
             scratch((2, micro, ext, channels), F32),
             scratch((micro, rows, channels), F32),
             scratch((micro, rows, channels), F32),
             scratch((3 * channels, channels), F32),
             scratch((2 * micro, channels), F32),
-            scratch((PARTS, nz, blk, cols), BF16),
-            scratch((PARTS, nz, blk, cols), BF16),
-            scratch((PARTS, ny, blk, cols), BF16),
+            scratch((PARTS, nz, sub, cols), BF16),
+            scratch((PARTS, nz, sub, cols), BF16),
+            scratch((PARTS, ny, sub, cols), BF16),
+            scratch((PARTS, nz, sub, cols), BF16),
+            scratch((3 * channels, channels), F32),
+            scratch((bins_count, 1, channels), F32),
+            scratch((bins_count, 1, channels), F32),
             scratch((nz, 2 * micro, channels), F32),
             scratch((ny, 2 * micro, channels), F32),
-            dma((6,)), dma((2,)), dma((2,)), dma((2,)), dma((2,)), dma((1,)), dma((1,)),
-            dma((own,)), dma((own,)), dma((2 * own,)), dma((2 * own,)),
-            dma((2 * own,)), dma((2 * own,)), dma((2 * own,)), dma((2 * own,)),
+            dma((4 + SPLIT,)), dma((units,)), dma((3,)),
+            dma((2,)), dma((2,)), dma((2,)), dma((2,)), dma((1,)), dma((1,)),
+            dma((own,)), dma((own,)), dma((units,)), dma((units,)),
+            dma((units,)), dma((units,)), dma((units,)), dma((units,)),
             dma((PARTS, nz)), dma((PARTS, nz)), dma((nz,)), dma((nz,)),
             dma((PARTS, ny)), dma((PARTS, ny)), dma((ny,)), dma((ny,)),
             dma((PARTS, nz)), dma((PARTS, nz)),
         ],
         compiler_params=pltpu.CompilerParams(
-            collective_id=0, has_side_effects=True, vmem_limit_bytes=48 * 1024 * 1024
+            collective_id=0, has_side_effects=True, vmem_limit_bytes=60 * 1024 * 1024
         ),
     )(activations, weights, gain_rows, shift_rows, doa_bins, cotangent)
     d_in, d_w, d_gain, d_shift = pl.pallas_call(
         finish_body,
         out_shape=(
             jax.ShapeDtypeStruct((1, micro, rows, channels), BF16),
-            jax.ShapeDtypeStruct((1, 3 * channels, channels), F32),
+            jax.ShapeDtypeStruct((1, 3, channels, channels), F32),
             jax.ShapeDtypeStruct((bins_count, 1, channels), F32),
             jax.ShapeDtypeStruct((bins_count, 1, channels), F32),
         ),
-        in_specs=[vmem, vmem, vmem, smem],
+        in_specs=[hbm, hbm, hbm, hbm],
         out_specs=(hbm, hbm, hbm, hbm),
         scratch_shapes=[
-            scratch((3 * channels, channels), F32),
+            scratch((micro, rows, channels), BF16),
+            scratch((3, channels, channels), F32),
             scratch((bins_count, 1, channels), F32),
             scratch((bins_count, 1, channels), F32),
-            dma((4,)),
+            dma((3 + micro + 2,)),
+            dma((3 + micro + 2,)),
         ],
-        compiler_params=pltpu.CompilerParams(vmem_limit_bytes=16 * 1024 * 1024),
-    )(d_in, w_sum, tiny, doa_bins)
+        compiler_params=pltpu.CompilerParams(vmem_limit_bytes=60 * 1024 * 1024),
+    )(*held)
     return (
         d_in,
-        d_w.reshape(1, 3, channels, channels),
+        d_w,
         jnp.transpose(d_gain, (1, 0, 2)),
         jnp.transpose(d_shift, (1, 0, 2)),
     )

time: 95.9 us -> 87.6 us (0.913)
  local copies, waits for them, and re-layouts: 5.26 us -> 0 us
  Pallas kernels: 89.6 us -> 86.2 us
    unnamed x12 -> x0, local copies, waits for them, and re-layouts: 5.26 us -> none
    pallas_call x1, Pallas kernels: 88 us -> 84 us  [shards(): pl.pallas_call(functools.partial(chain_body, sizes), out_shape=(jax.Shape...]
where the time goes in v3:
time: 87.6 us; the launch traced here: 86.8 us
  Pallas kernels  86.2 us (98%)
    pallas_call x1, Pallas kernels, shards(): pl.pallas_call(functools.partial(chain_body, sizes), out_shape=(jax.Shape...  84 us
    pallas_call x1, Pallas kernels, shards(): pl.pallas_call(finish_body, out_shape=(jax.ShapeDtypeStruct((1, micro, ro...  2.17 us

profile of v3, /device:TPU:1, one launch (start us, length us, event | category | flops | bytes accessed | tf_op | source)
XLA Modules:
  0.0 86.8 jit_solution(5018145262896300806)
XLA Ops:
  0.6 84.0 %shard_map.93 = (bf16[4,256,256]{2,1,0:T(8,128)(2,1)}, f32[768,256]{1,0:T(8,128)}, f32[36,1,256]{2,1,0:T(1,128)}, f32[36,1,256]{2,1,0:T(1,128)}) custom-call(bf16[1,4,256,256]{3,2,1,0:T(8,128)(2,1)} %x_ref.1, bf16[1,3,256,256]{3,2,1,0:T(8,128)(2,1)} %w_ref.1, f32[36,1,256]{2,1,0:T(1,128)} %bitcast.4, f32[36,1,256]{2,1,0:T(1,128)} %bitcast.5, s32[4]{0:T(128)} %bins_ref.1, ...), custom_call_target="tpu_custom_call" | custom-call | tf_op jit(solution)/shard_map/pallas_call | solution.py:467
  84.7 2.2 %shard_map.94 = (bf16[1,4,256,256]{3,2,1,0:T(8,128)(2,1)}, f32[1,3,256,256]{3,2,1,0:T(8,128)}, f32[36,1,256]{2,1,0:T(1,128)}, f32[36,1,256]{2,1,0:T(1,128)}) custom-call(bf16[4,256,256]{2,1,0:T(8,128)(2,1)} %get-tuple-element.12.din_ref, f32[768,256]{1,0:T(8,128)} %get-tuple-element.13.dw_ref, f32[36,1,256]{2,1,0:T(1,128)} %get-tuple-element.14.gain_ref, ...), custom_call_target="tpu_custom_call" | custom-call | tf_op jit(solution)/shard_map/pallas_call | solution.py:513

commit v4 on v3

--- a/solution.py
+++ b/solution.py
@@ -42,6 +42,7 @@
     cols = channels // COL_PARTS
     own_count = micro // 2
     units = SPLIT * own_count
+    middles = 2 * own_count
     z_order = sorted(range(1, nz), key=lambda k: -min(k, nz - k))
     y_order = sorted(range(1, ny), key=lambda k: -min(k, ny - k))
     s = lax.axis_index("section")
@@ -116,26 +117,6 @@
     for k in range(3):
         wt[c, k] = wv[k].astype(F32).T.astype(BF16)
 
-    chain_peers = jnp.where(passes_on, 1, 0) + jnp.where(later_chip, 1, 0)
-    pl.semaphore_wait(barrier, 3 + (nz - 1) + (ny - 1) + chain_peers)
-
-    def copy(src, dst, send, recv, to):
-        return pltpu.make_async_remote_copy(src_ref=src, dst_ref=dst, send_sem=send, recv_sem=recv, device_id=to, device_id_type=MESH)
-
-    x_right = copy(x_ref.at[0, :, pl.ds(rows - wide, wide)], xh.at[:, pl.ds(0, wide)], hx_s.at[0], hx_r.at[0], (s, right))
-    x_left = copy(x_ref.at[0, :, pl.ds(0, wide)], xh.at[:, pl.ds(wide + rows, wide)], hx_s.at[1], hx_r.at[1], (s, left))
-    c_right = copy(cot_ref.at[pl.ds(mine, own_count), pl.ds(rows - HALO, HALO)], hist.at[0, :, 0, pl.ds(0, HALO)], hc_s.at[0], hc_r.at[0], (s, right))
-    c_left = copy(cot_ref.at[pl.ds(mine, own_count), pl.ds(0, HALO)], hist.at[0, :, SPLIT - 1, pl.ds(unit - HALO, HALO)], hc_s.at[1], hc_r.at[1], (s, left))
-    w_peer = copy(wt.at[c], wt.at[c], wt_s.at[0], wt_r.at[0], (peer, b))
-    x_right.start()
-    x_left.start()
-
-    @pl.when(first_chip)
-    def _():
-        c_right.start()
-        c_left.start()
-
-    w_peer.start()
     for one in loads[1:]:
         one.wait()
 
@@ -149,7 +130,8 @@
         d = sig * (1.0 + filmed * (1.0 - sig))
         return d, d * gain
 
-    def inner(m, carry):
+    def inner(j, carry):
+        m = lax.rem(theirs + j, micro)
         pre = taps(xh[m, wide:wide + rows])
         d, full = film(pre, bins[m])
         dmat[c, m, HALO:HALO + rows] = full
@@ -157,15 +139,39 @@
         dpre[m] = d * pre
         return carry
 
-    lax.fori_loop(0, micro, inner, 0)
-    x_right.wait_recv()
-    x_left.wait_recv()
-
-    def d_copy(j):
-        m = theirs + j
-        return copy(dmat.at[c, m], dmat.at[c, m], d_s.at[j], d_r.at[j], (peer, b))
-
-    def forward(j, carry):
+    lax.fori_loop(0, own_count, inner, 0)
+
+    chain_peers = jnp.where(passes_on, 1, 0) + jnp.where(later_chip, 1, 0)
+    pl.semaphore_wait(barrier, 3 + (nz - 1) + (ny - 1) + chain_peers)
+
+    def copy(src, dst, send, recv, to):
+        return pltpu.make_async_remote_copy(src_ref=src, dst_ref=dst, send_sem=send, recv_sem=recv, device_id=to, device_id_type=MESH)
+
+    x_right = copy(x_ref.at[0, :, pl.ds(rows - wide, wide)], xh.at[:, pl.ds(0, wide)], hx_s.at[0], hx_r.at[0], (s, right))
+    x_left = copy(x_ref.at[0, :, pl.ds(0, wide)], xh.at[:, pl.ds(wide + rows, wide)], hx_s.at[1], hx_r.at[1], (s, left))
+    c_right = copy(cot_ref.at[pl.ds(mine, own_count), pl.ds(rows - HALO, HALO)], hist.at[0, :, 0, pl.ds(0, HALO)], hc_s.at[0], hc_r.at[0], (s, right))
+    c_left = copy(cot_ref.at[pl.ds(mine, own_count), pl.ds(0, HALO)], hist.at[0, :, SPLIT - 1, pl.ds(unit - HALO, HALO)], hc_s.at[1], hc_r.at[1], (s, left))
+    w_peer = copy(wt.at[c], wt.at[c], wt_s.at[0], wt_r.at[0], (peer, b))
+    d_spans = (pl.ds(wide, rows - wide), pl.ds(0, wide), pl.ds(rows, wide))
+
+    def d_copy(j, part):
+        at = dmat.at[c, theirs + j, d_spans[part]]
+        return copy(at, at, d_s.at[j, part], d_r.at[j, part], (peer, b))
+
+    x_right.start()
+    x_left.start()
+    for j in range(own_count):
+        d_copy(j, 0).start()
+    w_peer.start()
+
+    @pl.when(first_chip)
+    def _():
+        c_right.start()
+        c_left.start()
+
+    lax.fori_loop(own_count, micro, inner, 0)
+
+    def outer(j, carry):
         m = lax.rem(theirs + j, micro)
         ends = jnp.concatenate([xh[m, 0:2 * wide], xh[m, rows:rows + 2 * wide]], axis=0)
         pre = taps(ends)
@@ -177,7 +183,8 @@
 
         @pl.when(j < own_count)
         def _():
-            d_copy(j).start()
+            d_copy(j, 1).start()
+            d_copy(j, 2).start()
 
         both = d * pre
         dgrad[m, 0:HALO] = d[wide:wide + HALO]
@@ -186,7 +193,10 @@
         dpre[m, rows - HALO:rows] = both[high][0:HALO]
         return carry
 
-    lax.fori_loop(0, micro, forward, 0)
+    def ends_forward():
+        x_right.wait_recv()
+        x_left.wait_recv()
+        lax.fori_loop(0, micro, outer, 0)
 
     def turn(m, carry):
         xs = xh[m].astype(F32)
@@ -206,20 +216,24 @@
 
     @pl.when(later_chip)
     def _():
+        ends_forward()
         lax.fori_loop(0, micro, turn, 0)
 
     @pl.when(first_chip)
     def _():
         for one in cot_loads:
             one.wait()
-        c_right.wait_recv()
-        c_left.wait_recv()
 
     w_peer.wait_recv()
 
     def split(u):
-        i = u // SPLIT
-        return i, u - SPLIT * i
+        late = u // middles
+        side = u % 2
+        i = (u % middles) // 2
+        return i, (1 - late) * (1 + side) + late * (SPLIT - 1) * side
+
+    def units_of(i):
+        return [2 * i, 2 * i + 1, middles + 2 * i, middles + 2 * i + 1]
 
     def chain_copy(u):
         i, h = split(u)
@@ -256,9 +270,23 @@
         m, at = spot_of(u)
         span = pl.ds(pl.multiple_of(h * half, half), unit)
 
+        @pl.when(first_chip & (u == middles - 1))
+        def _():
+            ends_forward()
+
+        @pl.when(h == 1)
+        def _():
+            d_copy(i, 0).wait_recv()
+
         @pl.when(h == 0)
         def _():
-            d_copy(i).wait_recv()
+            d_copy(i, 1).wait_recv()
+            d_copy(i, 2).wait_recv()
+
+        @pl.when(first_chip & (u == middles))
+        def _():
+            c_right.wait_recv()
+            c_left.wait_recv()
 
         @pl.when(later_chip)
         def _():
@@ -284,8 +312,8 @@
 
         @pl.when(later_chip & (h == 0) & (i > 0))
         def _():
-            for k in range(SPLIT):
-                grad_copy(u - SPLIT + k).wait_recv()
+            for k in units_of(i - 1):
+                grad_copy(k).wait_recv()
             weight_step(theirs + i - 1)
 
         return carry
@@ -298,12 +326,12 @@
         for i in range(own_count):
             weight_step(mine + i)
         for i in range(own_count - 1):
-            for k in range(SPLIT):
-                grad_copy(SPLIT * i + k).wait_recv()
+            for k in units_of(i):
+                grad_copy(k).wait_recv()
             weight_step(theirs + i)
 
-    for k in range(SPLIT):
-        grad_copy(units - SPLIT + k).wait_recv()
+    for k in units_of(own_count - 1):
+        grad_copy(k).wait_recv()
     weight_step(theirs + own_count - 1)
 
     def scatter(q, k):
@@ -396,7 +424,8 @@
         c_left.wait_send()
 
     for j in range(own_count):
-        d_copy(j).wait_send()
+        for part in range(3):
+            d_copy(j, part).wait_send()
     for u in range(units):
         grad_copy(u).wait_send()
         out_copy(u).wait()
@@ -500,7 +529,7 @@
             scratch((ny, 2 * micro, channels), F32),
             dma((4 + SPLIT,)), dma((units,)), dma((3,)),
             dma((2,)), dma((2,)), dma((2,)), dma((2,)), dma((1,)), dma((1,)),
-            dma((own,)), dma((own,)), dma((units,)), dma((units,)),
+            dma((own, 3)), dma((own, 3)), dma((units,)), dma((units,)),
             dma((units,)), dma((units,)), dma((units,)), dma((units,)),
             dma((PARTS, nz)), dma((PARTS, nz)), dma((nz,)), dma((nz,)),
             dma((PARTS, ny)), dma((PARTS, ny)), dma((ny,)), dma((ny,)),

time: 87.6 us -> 85.3 us (0.974)
  Pallas kernels: 86.2 us -> 84.5 us
    pallas_call x1, Pallas kernels: 84 us -> 82.4 us  [shards(): pl.pallas_call(functools.partial(chain_body, sizes), out_shape=(jax.Shape...]
where the time goes in v4:
time: 85.3 us; the launch traced here: 85.2 us
  Pallas kernels  84.5 us (99%)
    pallas_call x1, Pallas kernels, shards(): pl.pallas_call(functools.partial(chain_body, sizes), out_shape=(jax.Shape...  82.4 us
    pallas_call x1, Pallas kernels, shards(): pl.pallas_call(finish_body, out_shape=(jax.ShapeDtypeStruct((1, micro, ro...  2.17 us

profile of v4, /device:TPU:1, one launch (start us, length us, event | category | flops | bytes accessed | tf_op | source)
XLA Modules:
  0.0 85.2 jit_solution(5875253123782016974)
XLA Ops:
  0.6 82.4 %shard_map.93 = (bf16[4,256,256]{2,1,0:T(8,128)(2,1)}, f32[768,256]{1,0:T(8,128)}, f32[36,1,256]{2,1,0:T(1,128)}, f32[36,1,256]{2,1,0:T(1,128)}) custom-call(bf16[1,4,256,256]{3,2,1,0:T(8,128)(2,1)} %x_ref.1, bf16[1,3,256,256]{3,2,1,0:T(8,128)(2,1)} %w_ref.1, f32[36,1,256]{2,1,0:T(1,128)} %bitcast.4, f32[36,1,256]{2,1,0:T(1,128)} %bitcast.5, s32[4]{0:T(128)} %bins_ref.1, ...), custom_call_target="tpu_custom_call" | custom-call | tf_op jit(solution)/shard_map/pallas_call | solution.py:496
  83.0 2.2 %shard_map.94 = (bf16[1,4,256,256]{3,2,1,0:T(8,128)(2,1)}, f32[1,3,256,256]{3,2,1,0:T(8,128)}, f32[36,1,256]{2,1,0:T(1,128)}, f32[36,1,256]{2,1,0:T(1,128)}) custom-call(bf16[4,256,256]{2,1,0:T(8,128)(2,1)} %get-tuple-element.12.din_ref, f32[768,256]{1,0:T(8,128)} %get-tuple-element.13.dw_ref, f32[36,1,256]{2,1,0:T(1,128)} %get-tuple-element.14.gain_ref, ...), custom_call_target="tpu_custom_call" | custom-call | tf_op jit(solution)/shard_map/pallas_call | solution.py:542

commit v5 on v4

--- a/solution.py
+++ b/solution.py
@@ -160,9 +160,10 @@
 
     x_right.start()
     x_left.start()
-    for j in range(own_count):
+    d_copy(0, 0).start()
+    w_peer.start()
+    for j in range(1, own_count):
         d_copy(j, 0).start()
-    w_peer.start()
 
     @pl.when(first_chip)
     def _():
@@ -202,17 +203,26 @@
         xs = xh[m].astype(F32)
         for j, sh in enumerate((1, 0, -1)):
             part = rolled(xs, sh) if sh else xs
-            xt[m, j * channels:(j + 1) * channels] = part[wide:wide + rows].T.astype(BF16)
+            xt[lax.rem(m, own_count), m // own_count, j * channels:(j + 1) * channels] = part[wide:wide + rows].T.astype(BF16)
         return carry
 
     acc[...] = jnp.zeros_like(acc)
 
-    def weight_step(m):
-        g = gown[m].astype(F32)
-        gp = (g * dmat[c, m, HALO:HALO + rows]).astype(BF16)
-        acc[...] += dot(xt[m], gp)
-        small[pl.ds(m, 1)] = jnp.sum(g * dpre[m], 0, keepdims=True)
-        small[pl.ds(micro + m, 1)] = jnp.sum(g * dgrad[m], 0, keepdims=True)
+    def pair_term(i):
+        both = []
+        for k in range(2):
+            m = own_count * k + i
+            g = gown[m].astype(F32)
+            both.append((g * dmat[c, m, HALO:HALO + rows]).astype(BF16))
+            small[pl.ds(m, 1)] = jnp.sum(g * dpre[m], 0, keepdims=True)
+            small[pl.ds(micro + m, 1)] = jnp.sum(g * dgrad[m], 0, keepdims=True)
+        left_side = jnp.concatenate([xt[i, 0], xt[i, 1]], axis=1)
+        return dot(left_side, jnp.concatenate(both, axis=0))
+
+    def weight_pair(i):
+        for k in units_of(i):
+            grad_copy(k).wait_recv()
+        acc[...] += pair_term(i)
 
     @pl.when(later_chip)
     def _():
@@ -235,9 +245,17 @@
     def units_of(i):
         return [2 * i, 2 * i + 1, middles + 2 * i, middles + 2 * i + 1]
 
-    def chain_copy(u):
+    def chain_copy(u, whole):
         i, h = split(u)
-        return copy(hist.at[2, i, h], hist.at[0, i, h], ch_s.at[u], ch_r.at[u], (s - 2, b))
+        at = pl.ds(0, unit) if whole else pl.ds(pl.multiple_of(h // 2 * HALO, HALO), unit - HALO)
+        return copy(hist.at[2, i, h, at], hist.at[0, i, h, at], ch_s.at[u], ch_r.at[u], (s - 2, b))
+
+    def side_halo(i, h):
+        upper_half = h // 2
+        to = pl.multiple_of((1 - upper_half) * (unit - HALO), HALO)
+        source = upper_half * (h - 1) + 1 - upper_half
+        start = pl.multiple_of(HALO + upper_half * (half - HALO), HALO)
+        hist[0, i, h, pl.ds(to, HALO)] = hist[0, i, source, pl.ds(start, HALO)]
 
     def spot_of(u):
         i, h = split(u)
@@ -288,33 +306,37 @@
             c_right.wait_recv()
             c_left.wait_recv()
 
-        @pl.when(later_chip)
-        def _():
-            chain_copy(u).wait_recv()
+        @pl.when(later_chip & (h == 1))
+        def _():
+            chain_copy(u, True).wait_recv()
+
+        @pl.when(later_chip & (h != 1))
+        def _():
+            chain_copy(u, False).wait_recv()
+            side_halo(i, h)
 
         upper = back(hist[0, i, h].astype(F32), 1, m, span)
         hist[1, i, h] = upper
+        grad_copy(u).start()
         lower = back(upper.astype(F32), 0, m, span)
         hist[2, i, h] = lower
 
-        @pl.when(passes_on)
-        def _():
-            chain_copy(u).start()
-
-        grad_copy(u).start()
+        @pl.when(passes_on & (h == 1))
+        def _():
+            chain_copy(u, True).start()
+
+        @pl.when(passes_on & (h != 1))
+        def _():
+            chain_copy(u, False).start()
+
         out_copy(u).start()
         own_copy(u).start()
         gown[m, at] = hist[1 - c, i, h, HALO:HALO + half]
 
-        @pl.when(later_chip & (h == SPLIT - 1))
-        def _():
-            weight_step(m)
-
-        @pl.when(later_chip & (h == 0) & (i > 0))
-        def _():
-            for k in units_of(i - 1):
-                grad_copy(k).wait_recv()
-            weight_step(theirs + i - 1)
+        for k in range(own_count - 1):
+            @pl.when(later_chip & (u == middles + 2 * k + 2))
+            def _():
+                weight_pair(k)
 
         return carry
 
@@ -323,16 +345,12 @@
     @pl.when(first_chip)
     def _():
         lax.fori_loop(0, micro, turn, 0)
-        for i in range(own_count):
-            weight_step(mine + i)
         for i in range(own_count - 1):
-            for k in units_of(i):
-                grad_copy(k).wait_recv()
-            weight_step(theirs + i)
+            weight_pair(i)
 
     for k in units_of(own_count - 1):
         grad_copy(k).wait_recv()
-    weight_step(theirs + own_count - 1)
+    last_term = pair_term(own_count - 1)
 
     def scatter(q, k):
         to = lax.rem(z + k, nz)
@@ -357,7 +375,7 @@
     for q in range(PARTS):
         for j in range(nz):
             at_rows, at_cols = area(q, j)
-            wpart[q, j] = acc[at_rows, at_cols].astype(BF16)
+            wpart[q, j] = (acc[at_rows, at_cols] + last_term[at_rows, at_cols]).astype(BF16)
         for k in z_order:
             scatter(q, k).start()
     for k in z_order:
@@ -434,7 +452,7 @@
     @pl.when(passes_on)
     def _():
         for u in range(units):
-            chain_copy(u).wait_send()
+            chain_copy(u, split(u)[1] == 1).wait_send()
 
     for k in range(1, nz):
         small_z(k).wait_send()
@@ -443,11 +461,12 @@
     for q in range(PARTS):
         for k in range(1, nz):
             gather(q, k).wait()
+        part, side = q // COL_PARTS, q % COL_PARTS
         for j in range(nz):
-            at_rows, at_cols = area(q, j)
-            wide_w[at_rows, at_cols] = wgather[q, j].astype(F32)
-    stores.append(pltpu.make_async_copy(wide_w, dw_ref, store_s.at[2]))
-    stores[2].start()
+            wide_w[j, part, :, side * cols:(side + 1) * cols] = wgather[q, j].astype(F32)
+        if side == COL_PARTS - 1:
+            stores.append(pltpu.make_async_copy(wide_w.at[:, part], dw_ref.at[:, part], store_s.at[2 + part]))
+            stores[-1].start()
     for one in stores:
         one.wait()
     for q in range(PARTS):
@@ -493,11 +512,11 @@
     scratch = pltpu.VMEM
     gain_rows = jnp.transpose(film_gain, (1, 0, 2))
     shift_rows = jnp.transpose(film_shift, (1, 0, 2))
-    held = pl.pallas_call(
+    d_in, d_w, d_gain, d_shift = pl.pallas_call(
         functools.partial(chain_body, sizes),
         out_shape=(
             jax.ShapeDtypeStruct((micro, rows, channels), BF16),
-            jax.ShapeDtypeStruct((3 * channels, channels), F32),
+            jax.ShapeDtypeStruct((nz, ROW_PARTS, sub, channels), F32),
             jax.ShapeDtypeStruct((bins_count, 1, channels), F32),
             jax.ShapeDtypeStruct((bins_count, 1, channels), F32),
         ),
@@ -507,7 +526,7 @@
             scratch((micro, ext + 2 * HALO, channels), BF16),
             scratch((3, channels, channels), BF16),
             scratch((2, 3, channels, channels), BF16),
-            scratch((micro, 3 * channels, rows), BF16),
+            scratch((own, 2, 3 * channels, rows), BF16),
             scratch((bins_count, 1, channels), F32),
             scratch((bins_count, 1, channels), F32),
             pltpu.SMEM((micro,), jnp.int32),
@@ -522,12 +541,12 @@
             scratch((PARTS, nz, sub, cols), BF16),
             scratch((PARTS, ny, sub, cols), BF16),
             scratch((PARTS, nz, sub, cols), BF16),
-            scratch((3 * channels, channels), F32),
+            scratch((nz, ROW_PARTS, sub, channels), F32),
             scratch((bins_count, 1, channels), F32),
             scratch((bins_count, 1, channels), F32),
             scratch((nz, 2 * micro, channels), F32),
             scratch((ny, 2 * micro, channels), F32),
-            dma((4 + SPLIT,)), dma((units,)), dma((3,)),
+            dma((4 + SPLIT,)), dma((units,)), dma((2 + ROW_PARTS,)),
             dma((2,)), dma((2,)), dma((2,)), dma((2,)), dma((1,)), dma((1,)),
             dma((own, 3)), dma((own, 3)), dma((units,)), dma((units,)),
             dma((units,)), dma((units,)), dma((units,)), dma((units,)),
@@ -558,7 +577,7 @@
             dma((3 + micro + 2,)),
         ],
         compiler_params=pltpu.CompilerParams(vmem_limit_bytes=60 * 1024 * 1024),
-    )(*held)
+    )(d_in, d_w.reshape(3 * channels, channels), d_gain, d_shift)
     return (
         d_in,
         d_w,

time: 85.3 us -> 81.7 us (0.958)
  Pallas kernels: 84.5 us -> 80.9 us
    pallas_call x1, Pallas kernels: 82.4 us -> 78.7 us  [shards(): pl.pallas_call(functools.partial(chain_body, sizes), out_shape=(jax.Shape...]
where the time goes in v5:
time: 81.7 us; the launch traced here: 81.5 us
  Pallas kernels  80.9 us (99%)
    pallas_call x1, Pallas kernels, shards(): pl.pallas_call(functools.partial(chain_body, sizes), out_shape=(jax.Shape...  78.7 us
    pallas_call x1, Pallas kernels, shards(): pl.pallas_call(finish_body, out_shape=(jax.ShapeDtypeStruct((1, micro, ro...  2.17 us

profile of v5, /device:TPU:1, one launch (start us, length us, event | category | flops | bytes accessed | tf_op | source)
XLA Modules:
  0.0 81.5 jit_solution(12475309098143286189)
XLA Ops:
  0.6 78.7 %shard_map.93 = (bf16[4,256,256]{2,1,0:T(8,128)(2,1)}, f32[8,2,48,256]{3,2,1,0:T(8,128)}, f32[36,1,256]{2,1,0:T(1,128)}, f32[36,1,256]{2,1,0:T(1,128)}) custom-call(bf16[1,4,256,256]{3,2,1,0:T(8,128)(2,1)} %x_ref.1, bf16[1,3,256,256]{3,2,1,0:T(8,128)(2,1)} %w_ref.1, f32[36,1,256]{2,1,0:T(1,128)} %bitcast.6, f32[36,1,256]{2,1,0:T(1,128)} %bitcast.7, ...), custom_call_target="tpu_custom_call" | custom-call | tf_op jit(solution)/shard_map/pallas_call | solution.py:515
  79.3 2.2 %shard_map.94 = (bf16[1,4,256,256]{3,2,1,0:T(8,128)(2,1)}, f32[1,3,256,256]{3,2,1,0:T(8,128)}, f32[36,1,256]{2,1,0:T(1,128)}, f32[36,1,256]{2,1,0:T(1,128)}) custom-call(bf16[4,256,256]{2,1,0:T(8,128)(2,1)} %get-tuple-element.12.din_ref, f32[768,256]{1,0:T(8,128)} %bitcast.5, f32[36,1,256]{2,1,0:T(1,128)} %get-tuple-element.14.gain_ref, ...), custom_call_target="tpu_custom_call" | custom-call | tf_op jit(solution)/shard_map/pallas_call | solution.py:561

commit v6 on v5

--- a/solution.py
+++ b/solution.py
@@ -172,32 +172,32 @@
 
     lax.fori_loop(own_count, micro, inner, 0)
 
-    def outer(j, carry):
+    def outer(j, pre):
         m = lax.rem(theirs + j, micro)
-        ends = jnp.concatenate([xh[m, 0:2 * wide], xh[m, rows:rows + 2 * wide]], axis=0)
-        pre = taps(ends)
         d, full = film(pre, bins[m])
         low = slice(HALO, HALO + wide)
         high = slice(2 * wide + HALO, 3 * wide + HALO)
         dmat[c, m, 0:wide] = full[low]
         dmat[c, m, rows:rows + wide] = full[high]
-
-        @pl.when(j < own_count)
-        def _():
+        if j < own_count:
             d_copy(j, 1).start()
             d_copy(j, 2).start()
-
         both = d * pre
         dgrad[m, 0:HALO] = d[wide:wide + HALO]
         dpre[m, 0:HALO] = both[wide:wide + HALO]
         dgrad[m, rows - HALO:rows] = d[high][0:HALO]
         dpre[m, rows - HALO:rows] = both[high][0:HALO]
-        return carry
 
     def ends_forward():
         x_right.wait_recv()
         x_left.wait_recv()
-        lax.fori_loop(0, micro, outer, 0)
+        ends = []
+        for j in range(micro):
+            m = lax.rem(theirs + j, micro)
+            ends += [xh[m, 0:2 * wide], xh[m, rows:rows + 2 * wide]]
+        pre = taps(jnp.concatenate(ends, axis=0))
+        for j in range(micro):
+            outer(j, pre[4 * wide * j:4 * wide * (j + 1)])
 
     def turn(m, carry):
         xs = xh[m].astype(F32)
@@ -247,34 +247,30 @@
 
     def chain_copy(u, whole):
         i, h = split(u)
-        at = pl.ds(0, unit) if whole else pl.ds(pl.multiple_of(h // 2 * HALO, HALO), unit - HALO)
+        at = pl.ds(0, unit) if whole else pl.ds(h // 2 * HALO, unit - HALO)
         return copy(hist.at[2, i, h, at], hist.at[0, i, h, at], ch_s.at[u], ch_r.at[u], (s - 2, b))
 
     def side_halo(i, h):
         upper_half = h // 2
-        to = pl.multiple_of((1 - upper_half) * (unit - HALO), HALO)
+        to = (1 - upper_half) * (unit - HALO)
         source = upper_half * (h - 1) + 1 - upper_half
-        start = pl.multiple_of(HALO + upper_half * (half - HALO), HALO)
+        start = HALO + upper_half * (half - HALO)
         hist[0, i, h, pl.ds(to, HALO)] = hist[0, i, source, pl.ds(start, HALO)]
 
     def spot_of(u):
         i, h = split(u)
-        return mine + i, pl.ds(pl.multiple_of(h * half, half), half)
+        return mine + i, pl.ds(h * half, half)
 
     def grad_copy(u):
         i, h = split(u)
         m, at = spot_of(u)
         return copy(hist.at[c, i, h, pl.ds(HALO, half)], gown.at[m, at], pa_s.at[u], pa_r.at[u], (peer, b))
 
-    def out_copy(u):
-        i, h = split(u)
-        m, at = spot_of(u)
-        return copy(hist.at[c + 1, i, h, pl.ds(HALO, half)], din_ref.at[m, at], pb_s.at[u], pb_r.at[u], (peer, b))
-
-    def own_copy(u):
-        i, h = split(u)
-        m, at = spot_of(u)
-        return pltpu.make_async_copy(hist.at[2 - c, i, h, pl.ds(HALO, half)], din_ref.at[m, at], own_s.at[u])
+    def out_copy(i):
+        return copy(hist.at[c + 1, i, :, pl.ds(HALO, half)], din_ref.at[mine + i], pb_s.at[i], pb_r.at[i], (peer, b))
+
+    def own_copy(i):
+        return pltpu.make_async_copy(hist.at[2 - c, i, :, pl.ds(HALO, half)], din_ref.at[mine + i], own_s.at[i])
 
     def back(g, sec, m, at):
         gp = (g * dmat[sec, m, at]).astype(BF16)
@@ -283,64 +279,60 @@
         out = out + rolled(dot(gp, wt[sec, 2]), 1)
         return out.astype(BF16)
 
-    def chain(u, carry):
+    def chain(u):
         i, h = split(u)
         m, at = spot_of(u)
-        span = pl.ds(pl.multiple_of(h * half, half), unit)
-
-        @pl.when(first_chip & (u == middles - 1))
-        def _():
-            ends_forward()
-
-        @pl.when(h == 1)
-        def _():
+        span = pl.ds(h * half, unit)
+        if u == middles - 1:
+            @pl.when(first_chip)
+            def _():
+                ends_forward()
+
+        if h == 1:
             d_copy(i, 0).wait_recv()
-
-        @pl.when(h == 0)
-        def _():
+        if h == 0:
             d_copy(i, 1).wait_recv()
             d_copy(i, 2).wait_recv()
-
-        @pl.when(first_chip & (u == middles))
+        if u == middles:
+            @pl.when(first_chip)
+            def _():
+                c_right.wait_recv()
+                c_left.wait_recv()
+
+        @pl.when(later_chip)
         def _():
-            c_right.wait_recv()
-            c_left.wait_recv()
-
-        @pl.when(later_chip & (h == 1))
-        def _():
-            chain_copy(u, True).wait_recv()
-
-        @pl.when(later_chip & (h != 1))
-        def _():
-            chain_copy(u, False).wait_recv()
-            side_halo(i, h)
+            chain_copy(u, h == 1).wait_recv()
+            if h != 1:
+                side_halo(i, h)
 
         upper = back(hist[0, i, h].astype(F32), 1, m, span)
         hist[1, i, h] = upper
-        grad_copy(u).start()
+
+        @pl.when(jnp.logical_not(passes_on))
+        def _():
+            grad_copy(u).start()
+
         lower = back(upper.astype(F32), 0, m, span)
         hist[2, i, h] = lower
 
-        @pl.when(passes_on & (h == 1))
+        @pl.when(passes_on)
         def _():
-            chain_copy(u, True).start()
-
-        @pl.when(passes_on & (h != 1))
-        def _():
-            chain_copy(u, False).start()
-
-        out_copy(u).start()
-        own_copy(u).start()
+            chain_copy(u, h == 1).start()
+            grad_copy(u).start()
+
+        if u >= middles and u % 2:
+            out_copy(i).start()
+            own_copy(i).start()
         gown[m, at] = hist[1 - c, i, h, HALO:HALO + half]
 
-        for k in range(own_count - 1):
-            @pl.when(later_chip & (u == middles + 2 * k + 2))
+        k = (u - middles) // 2 - 1
+        if u % 2 == 0 and 0 <= k < own_count - 1:
+            @pl.when(later_chip)
             def _():
                 weight_pair(k)
 
-        return carry
-
-    lax.fori_loop(0, units, chain, 0)
+    for u in range(units):
+        chain(u)
 
     @pl.when(first_chip)
     def _():
@@ -446,8 +438,9 @@
             d_copy(j, part).wait_send()
     for u in range(units):
         grad_copy(u).wait_send()
-        out_copy(u).wait()
-        own_copy(u).wait()
+    for i in range(own_count):
+        out_copy(i).wait()
+        own_copy(i).wait()
 
     @pl.when(passes_on)
     def _():
@@ -515,7 +508,7 @@
     d_in, d_w, d_gain, d_shift = pl.pallas_call(
         functools.partial(chain_body, sizes),
         out_shape=(
-            jax.ShapeDtypeStruct((micro, rows, channels), BF16),
+            jax.ShapeDtypeStruct((micro, SPLIT, rows // SPLIT, channels), BF16),
             jax.ShapeDtypeStruct((nz, ROW_PARTS, sub, channels), F32),
             jax.ShapeDtypeStruct((bins_count, 1, channels), F32),
             jax.ShapeDtypeStruct((bins_count, 1, channels), F32),
@@ -546,10 +539,10 @@
             scratch((bins_count, 1, channels), F32),
             scratch((nz, 2 * micro, channels), F32),
             scratch((ny, 2 * micro, channels), F32),
-            dma((4 + SPLIT,)), dma((units,)), dma((2 + ROW_PARTS,)),
+            dma((4 + SPLIT,)), dma((own,)), dma((2 + ROW_PARTS,)),
             dma((2,)), dma((2,)), dma((2,)), dma((2,)), dma((1,)), dma((1,)),
             dma((own, 3)), dma((own, 3)), dma((units,)), dma((units,)),
-            dma((units,)), dma((units,)), dma((units,)), dma((units,)),
+            dma((units,)), dma((units,)), dma((own,)), dma((own,)),
             dma((PARTS, nz)), dma((PARTS, nz)), dma((nz,)), dma((nz,)),
             dma((PARTS, ny)), dma((PARTS, ny)), dma((ny,)), dma((ny,)),
             dma((PARTS, nz)), dma((PARTS, nz)),
@@ -577,7 +570,7 @@
             dma((3 + micro + 2,)),
         ],
         compiler_params=pltpu.CompilerParams(vmem_limit_bytes=60 * 1024 * 1024),
-    )(d_in, d_w.reshape(3 * channels, channels), d_gain, d_shift)
+    )(d_in.reshape(micro, rows, channels), d_w.reshape(3 * channels, channels), d_gain, d_shift)
     return (
         d_in,
         d_w,

time: 81.7 us -> 82 us (level)
  no operation moved by 1% of the time
where the time goes in v6:
time: 82 us; the launch traced here: 81.8 us
  Pallas kernels  81.2 us (99%)
    pallas_call x1, Pallas kernels, shards(): pl.pallas_call(functools.partial(chain_body, sizes), out_shape=(jax.Shape...  79 us
    pallas_call x1, Pallas kernels, shards(): pl.pallas_call(finish_body, out_shape=(jax.ShapeDtypeStruct((1, micro, ro...  2.17 us

profile of v6, /device:TPU:1, one launch (start us, length us, event | category | flops | bytes accessed | tf_op | source)
XLA Modules:
  0.0 81.8 jit_solution(16654024887473925271)
XLA Ops:
  0.6 79.0 %shard_map.93 = (bf16[4,4,64,256]{3,2,1,0:T(8,128)(2,1)}, f32[8,2,48,256]{3,2,1,0:T(8,128)}, f32[36,1,256]{2,1,0:T(1,128)}, f32[36,1,256]{2,1,0:T(1,128)}) custom-call(bf16[1,4,256,256]{3,2,1,0:T(8,128)(2,1)} %x_ref.1, bf16[1,3,256,256]{3,2,1,0:T(8,128)(2,1)} %w_ref.1, f32[36,1,256]{2,1,0:T(1,128)} %bitcast.8, f32[36,1,256]{2,1,0:T(1,128)} %bitcast.9, ...), custom_call_target="tpu_custom_call" | custom-call | tf_op jit(solution)/shard_map/pallas_call | solution.py:508
  79.7 2.2 %shard_map.94 = (bf16[1,4,256,256]{3,2,1,0:T(8,128)(2,1)}, f32[1,3,256,256]{3,2,1,0:T(8,128)}, f32[36,1,256]{2,1,0:T(1,128)}, f32[36,1,256]{2,1,0:T(1,128)}) custom-call(bf16[4,256,256]{2,1,0:T(8,128)(2,1)} %bitcast.7, f32[768,256]{1,0:T(8,128)} %bitcast.6, f32[36,1,256]{2,1,0:T(1,128)} %get-tuple-element.14.gain_ref, f32[36,1,256]{2,1,0:T(1,128)} %get-tuple-element.15.shift_ref), custom_call_target="tpu_custom_call" | custom-call | tf_op jit(solution)/shard_map/pallas_call | solution.py:554

commit v7 on v6

--- a/solution.py
+++ b/solution.py
@@ -28,7 +28,7 @@
 def chain_body(sizes, x_ref, w_ref, gain_ref, shift_ref, bins_ref, cot_ref,
                din_ref, dw_ref, gain_out, shift_out,
                xh, wv, wt, xt, gainv, shiftv, bins, hist, gown, dmat, dgrad, dpre, acc, small,
-               wpart, wland, wsum, wgather, wide_w, gains, shifts, sland, ssum,
+               wpart, wland, wsum, wgather, gains, shifts, sland, ssum,
                load_s, own_s, store_s, hx_s, hx_r, hc_s, hc_r, wt_s, wt_r, d_s, d_r, ch_s, ch_r, pa_s, pa_r, pb_s, pb_r,
                z_s, z_r, zs_s, zs_r, y_s, y_r, ys_s, ys_r, ag_s, ag_r):
     sections, nz, ny, micro, rows, channels = sizes
@@ -65,28 +65,6 @@
     def y_peer(k):
         return lax.rem(y + k, ny) * nz + z
 
-    barrier = pltpu.get_barrier_semaphore()
-
-    def greet(sec, blk_id):
-        pl.semaphore_signal(barrier, inc=1, device_id=(sec, blk_id), device_id_type=MESH)
-
-    greet(s, left)
-    greet(s, right)
-    greet(peer, b)
-
-    @pl.when(passes_on)
-    def _():
-        greet(s - 2, b)
-
-    @pl.when(later_chip)
-    def _():
-        greet(s + 2, b)
-
-    for k in range(1, ny):
-        greet(s, y_peer(k))
-    for k in range(1, nz):
-        greet(s, z_peer(k))
-
     def local(src, dst, k):
         return pltpu.make_async_copy(src, dst, load_s.at[k])
 
@@ -110,6 +88,28 @@
     def _():
         for one in cot_loads:
             one.start()
+
+    barrier = pltpu.get_barrier_semaphore()
+
+    def greet(sec, blk_id):
+        pl.semaphore_signal(barrier, inc=1, device_id=(sec, blk_id), device_id_type=MESH)
+
+    greet(s, left)
+    greet(s, right)
+    greet(peer, b)
+
+    @pl.when(passes_on)
+    def _():
+        greet(s - 2, b)
+
+    @pl.when(later_chip)
+    def _():
+        greet(s + 2, b)
+
+    for k in range(1, ny):
+        greet(s, y_peer(k))
+    for k in range(1, nz):
+        greet(s, z_peer(k))
 
     for m in range(micro):
         bins[m] = bins_ref[m]
@@ -454,12 +454,8 @@
     for q in range(PARTS):
         for k in range(1, nz):
             gather(q, k).wait()
-        part, side = q // COL_PARTS, q % COL_PARTS
-        for j in range(nz):
-            wide_w[j, part, :, side * cols:(side + 1) * cols] = wgather[q, j].astype(F32)
-        if side == COL_PARTS - 1:
-            stores.append(pltpu.make_async_copy(wide_w.at[:, part], dw_ref.at[:, part], store_s.at[2 + part]))
-            stores[-1].start()
+        stores.append(pltpu.make_async_copy(wgather.at[q], dw_ref.at[q], store_s.at[2 + q]))
+        stores[-1].start()
     for one in stores:
         one.wait()
     for q in range(PARTS):
@@ -469,20 +465,28 @@
             across(q, k).wait_send()
 
 
-def finish_body(din_ref, dw_ref, gain_ref, shift_ref, din_out, dw_out, gain_out, shift_out, din, dw, gains, shifts, load_s, store_s):
+def finish_body(din_ref, dw_ref, gain_ref, shift_ref, din_out, dw_out, gain_out, shift_out, din, dw, wide_w, gains, shifts, load_s, store_s):
     micro = din_ref.shape[0]
-    tap = dw_ref.shape[0] // 3
-    trips = [(dw_ref.at[pl.ds(k * tap, tap)], dw.at[k], dw_out.at[0, k]) for k in range(3)]
-    trips += [(din_ref.at[m], din.at[m], din_out.at[0, m]) for m in range(micro)]
+    nz, cols = dw_ref.shape[1], dw_ref.shape[3]
+    w_loads = [pltpu.make_async_copy(dw_ref.at[q], dw.at[q], load_s.at[q]) for q in range(PARTS)]
+    w_stores = [pltpu.make_async_copy(wide_w.at[:, r], dw_out.at[:, r], store_s.at[r]) for r in range(ROW_PARTS)]
+    trips = [(din_ref.at[m], din.at[m], din_out.at[0, m]) for m in range(micro)]
     trips += [(gain_ref, gains, gain_out), (shift_ref, shifts, shift_out)]
-    loads = [pltpu.make_async_copy(src, mid, load_s.at[k]) for k, (src, mid, _) in enumerate(trips)]
-    stores = [pltpu.make_async_copy(mid, dst, store_s.at[k]) for k, (_, mid, dst) in enumerate(trips)]
-    for one in loads:
+    loads = [pltpu.make_async_copy(src, mid, load_s.at[PARTS + k]) for k, (src, mid, _) in enumerate(trips)]
+    stores = [pltpu.make_async_copy(mid, dst, store_s.at[ROW_PARTS + k]) for k, (_, mid, dst) in enumerate(trips)]
+    for one in w_loads + loads:
         one.start()
+    for q in range(PARTS):
+        w_loads[q].wait()
+        part, side = q // COL_PARTS, q % COL_PARTS
+        for j in range(nz):
+            wide_w[j, part, :, side * cols:(side + 1) * cols] = dw[q, j].astype(F32)
+        if side == COL_PARTS - 1:
+            w_stores[part].start()
     for one, two in zip(loads, stores):
         one.wait()
         two.start()
-    for two in stores:
+    for two in w_stores + stores:
         two.wait()
 
 
@@ -509,7 +513,7 @@
         functools.partial(chain_body, sizes),
         out_shape=(
             jax.ShapeDtypeStruct((micro, SPLIT, rows // SPLIT, channels), BF16),
-            jax.ShapeDtypeStruct((nz, ROW_PARTS, sub, channels), F32),
+            jax.ShapeDtypeStruct((PARTS, nz, sub, cols), BF16),
             jax.ShapeDtypeStruct((bins_count, 1, channels), F32),
             jax.ShapeDtypeStruct((bins_count, 1, channels), F32),
         ),
@@ -534,12 +538,11 @@
             scratch((PARTS, nz, sub, cols), BF16),
             scratch((PARTS, ny, sub, cols), BF16),
             scratch((PARTS, nz, sub, cols), BF16),
-            scratch((nz, ROW_PARTS, sub, channels), F32),
             scratch((bins_count, 1, channels), F32),
             scratch((bins_count, 1, channels), F32),
             scratch((nz, 2 * micro, channels), F32),
             scratch((ny, 2 * micro, channels), F32),
-            dma((4 + SPLIT,)), dma((own,)), dma((2 + ROW_PARTS,)),
+            dma((4 + SPLIT,)), dma((own,)), dma((2 + PARTS,)),
             dma((2,)), dma((2,)), dma((2,)), dma((2,)), dma((1,)), dma((1,)),
             dma((own, 3)), dma((own, 3)), dma((units,)), dma((units,)),
             dma((units,)), dma((units,)), dma((own,)), dma((own,)),
@@ -555,7 +558,7 @@
         finish_body,
         out_shape=(
             jax.ShapeDtypeStruct((1, micro, rows, channels), BF16),
-            jax.ShapeDtypeStruct((1, 3, channels, channels), F32),
+            jax.ShapeDtypeStruct((nz, ROW_PARTS, sub, channels), F32),
             jax.ShapeDtypeStruct((bins_count, 1, channels), F32),
             jax.ShapeDtypeStruct((bins_count, 1, channels), F32),
         ),
@@ -563,17 +566,18 @@
         out_specs=(hbm, hbm, hbm, hbm),
         scratch_shapes=[
             scratch((micro, rows, channels), BF16),
-            scratch((3, channels, channels), F32),
+            scratch((PARTS, nz, sub, cols), BF16),
+            scratch((nz, ROW_PARTS, sub, channels), F32),
             scratch((bins_count, 1, channels), F32),
             scratch((bins_count, 1, channels), F32),
-            dma((3 + micro + 2,)),
-            dma((3 + micro + 2,)),
+            dma((PARTS + micro + 2,)),
+            dma((ROW_PARTS + micro + 2,)),
         ],
         compiler_params=pltpu.CompilerParams(vmem_limit_bytes=60 * 1024 * 1024),
-    )(d_in.reshape(micro, rows, channels), d_w.reshape(3 * channels, channels), d_gain, d_shift)
+    )(d_in.reshape(micro, rows, channels), d_w, d_gain, d_shift)
     return (
         d_in,
-        d_w,
+        d_w.reshape(1, 3, channels, channels),
         jnp.transpose(d_gain, (1, 0, 2)),
         jnp.transpose(d_shift, (1, 0, 2)),
     )

time: 82 us -> 81.4 us (level)
  no operation moved by 1% of the time
where the time goes in v7:
time: 81.4 us; the launch traced here: 81.3 us
  Pallas kernels  80.6 us (99%)
    pallas_call x1, Pallas kernels, shards(): pl.pallas_call(functools.partial(chain_body, sizes), out_shape=(jax.Shape...  78.4 us
    pallas_call x1, Pallas kernels, shards(): pl.pallas_call(finish_body, out_shape=(jax.ShapeDtypeStruct((1, micro, ro...  2.17 us

profile of v7, /device:TPU:1, one launch (start us, length us, event | category | flops | bytes accessed | tf_op | source)
XLA Modules:
  0.0 81.3 jit_solution(10968202806088097919)
XLA Ops:
  0.6 78.4 %shard_map.93 = (bf16[4,4,64,256]{3,2,1,0:T(8,128)(2,1)}, bf16[4,8,48,128]{3,2,1,0:T(8,128)(2,1)}, f32[36,1,256]{2,1,0:T(1,128)}, f32[36,1,256]{2,1,0:T(1,128)}) custom-call(bf16[1,4,256,256]{3,2,1,0:T(8,128)(2,1)} %x_ref.1, bf16[1,3,256,256]{3,2,1,0:T(8,128)(2,1)} %w_ref.1, f32[36,1,256]{2,1,0:T(1,128)} %bitcast.7, f32[36,1,256]{2,1,0:T(1,128)} %bitcast.8, ...), custom_call_target="tpu_custom_call" | custom-call | tf_op jit(solution)/shard_map/pallas_call | solution.py:512
  79.1 2.2 %shard_map.94 = (bf16[1,4,256,256]{3,2,1,0:T(8,128)(2,1)}, f32[8,2,48,256]{3,2,1,0:T(8,128)}, f32[36,1,256]{2,1,0:T(1,128)}, f32[36,1,256]{2,1,0:T(1,128)}) custom-call(bf16[4,256,256]{2,1,0:T(8,128)(2,1)} %bitcast.6, bf16[4,8,48,128]{3,2,1,0:T(8,128)(2,1)} %get-tuple-element.13.dw_ref, f32[36,1,256]{2,1,0:T(1,128)} %get-tuple-element.14.gain_ref, ...), custom_call_target="tpu_custom_call" | custom-call | tf_op jit(solution)/shard_map/pallas_call | solution.py:557
